TPU v7x, 512 devices: a whole 4x4x16 slice. The times are simulated.
512 devices in a mesh: row: 128 (over y, x, z_lo, core), col: 4 (over z_hi).
Axes of the slice: x: 4, y: 4, z: 16 (z_hi: 4, z_lo: 4; z = z_hi * 4 + z_lo), core: 2. Of those that a mesh axis runs over, the one named last changes fastest.
Arguments:
- homolog_matrix: bfloat16 [256, 128, 4, 1, 256], P('row', None, 'col'), may hold values from -6 to 6
- pairs: bfloat16 [512, 128, 4, 1, 128], P('row', None, 'col'), may hold values from -6 to 6
- row_attention_weights: bfloat16 [256, 1024], replicated, may hold values from -2 to 2
- horizontal_projector: bfloat16 [256, 256], replicated, may hold values from -0.375 to 0.375
- pair_bias: bfloat16 [128, 8], replicated, may hold values from -0.5 to 0.5
- column_project: bfloat16 [256, 1024], replicated, may hold values from -2 to 2
- vertical_projector: bfloat16 [256, 256], replicated, may hold values from -0.375 to 0.375
- tensor_pair_maps: bfloat16 [256, 64], replicated, may hold values from -0.375 to 0.375
- outer_output: bfloat16 [1024, 128], replicated, may hold values from -1 to 1
- outgoing_project: bfloat16 [128, 640], replicated, may hold values from -0.5 to 0.5
- outgoing_output: bfloat16 [128, 128], replicated, may hold values from -0.5 to 0.5
- incoming_project: bfloat16 [128, 640], replicated, may hold values from -0.5 to 0.5
- incoming_output: bfloat16 [128, 128], replicated, may hold values from -0.5 to 0.5
Outputs:
- revised_homolog_matrix: bfloat16 [256, 128, 4, 1, 256], P('row', None, 'col')
- new_pairs: float32 [512, 128, 4, 1, 128], P('row', None, 'col')
All inputs are finite; a program needn't handle non-finite values.
Results may differ from a plain program's by a relative error of at most 0.018.
Values may be sent and summed in bfloat16 or wider, within the bound.
A program may use at most 64 MiB of HBM per device.

v0:
```python
import math

import jax
import jax.numpy as jnp
from jax import lax
from jax.sharding import PartitionSpec as P

HEAD_NUMBER = 8
HEAD_BREADTH = 32
OUTER_CHANNELS = 32
C_TRI = 128


EPS = 1e-05


def shortened(array):
    return jax.tree.map(lambda a: a.astype(jnp.bfloat16) if a.dtype == jnp.float32 else a, array)


def normalized_state(values, along=-1):
    values = values.astype(jnp.float32)
    center = values - jnp.mean(values, axis=along, keepdims=True)
    spread = jnp.mean(center * center, axis=along, keepdims=True)
    return center * lax.rsqrt(spread + EPS)


def shards(
    homolog_matrix,
    pairs,
    row_attention_weights,
    horizontal_projector,
    pair_bias,
    column_project,
    vertical_projector,
    tensor_pair_maps,
    outer_output,
    outgoing_project,
    outgoing_output,
    incoming_project,
    incoming_output,
):
    count_of_rows = lax.axis_size("row")
    col_count = lax.axis_size("col")
    local_sequences = homolog_matrix.shape[0]
    block_length = homolog_matrix.shape[3]
    alignment_width = homolog_matrix.shape[4]
    pair_rows = pairs.shape[0]
    pair_width = pairs.shape[4]
    local_heads = HEAD_NUMBER // col_count
    residues = pair_rows * count_of_rows
    local_columns = count_of_rows * block_length
    pair_normed = (
        normalized_state(pairs).astype(jnp.bfloat16).reshape(pair_rows * local_columns, pair_width)
    )
    bias_local = jnp.dot(pair_normed, pair_bias, preferred_element_type=jnp.float32).astype(
        jnp.bfloat16
    )
    bias_heads = bias_local.T.reshape(HEAD_NUMBER, pair_rows, count_of_rows, 1, block_length)
    spread_bias = lax.all_to_all(bias_heads, "col", split_axis=0, concat_axis=3, tiled=True)
    full_bias = lax.all_gather(spread_bias, "row", axis=1, tiled=True)
    full_bias = full_bias.reshape(local_heads, residues, residues)
    homolog_lines = homolog_matrix.reshape(local_sequences, local_columns, alignment_width)
    projected = jnp.dot(
        normalized_state(homolog_lines).astype(jnp.bfloat16),
        row_attention_weights,
        preferred_element_type=jnp.float32,
    ).astype(jnp.bfloat16)
    projected = projected.reshape(
        local_sequences, count_of_rows, 1, block_length, HEAD_NUMBER, 4 * HEAD_BREADTH
    )
    segment_list = lax.all_to_all(projected, "col", split_axis=4, concat_axis=2, tiled=True)
    element_count = segment_list.shape[0]
    flattened = segment_list.reshape(element_count, residues, local_heads, 4, HEAD_BREADTH)

    def one_sequence(sequence):
        query_rows = sequence[:, :, 0]
        key_rows = sequence[:, :, 1]
        value_rows = sequence[:, :, 2]
        gate_rows = sequence[:, :, 3]
        scores = jnp.einsum(
            "ihd,jhd->hij", query_rows, key_rows, preferred_element_type=jnp.float32
        ) / math.sqrt(HEAD_BREADTH)
        scores = scores + full_bias.astype(jnp.float32)
        weights = jax.nn.softmax(scores, axis=-1).astype(jnp.bfloat16)
        mixture = jnp.einsum(
            "hij,jhd->ihd", weights, value_rows, preferred_element_type=jnp.float32
        )
        gating = jax.nn.sigmoid(gate_rows.astype(jnp.float32))
        outputs = [(gating * mixture).astype(jnp.bfloat16)]
        return jnp.concatenate(outputs, axis=0)

    gated = lax.map(one_sequence, flattened)
    gated = gated.reshape(
        element_count, count_of_rows, col_count, block_length, local_heads * HEAD_BREADTH
    )
    returned_rows = lax.all_to_all(
        shortened(gated), "col", split_axis=2, concat_axis=4, tiled=True
    ).astype(gated.dtype)
    state_increment = jnp.dot(
        returned_rows.reshape(local_sequences, local_columns, HEAD_NUMBER * HEAD_BREADTH),
        horizontal_projector,
        preferred_element_type=jnp.float32,
    )
    state_after_rows = (homolog_lines.astype(jnp.float32) + state_increment).astype(jnp.bfloat16)
    state_after_rows = state_after_rows.reshape(
        local_sequences, count_of_rows, 1, block_length, alignment_width
    )
    segment_list = lax.all_to_all(state_after_rows, "row", split_axis=1, concat_axis=0, tiled=True)
    attend_seq_total = segment_list.shape[0]
    element_count = segment_list.shape[3]
    column_list = segment_list.reshape(attend_seq_total, element_count, alignment_width)
    combined = jnp.dot(
        normalized_state(column_list).astype(jnp.bfloat16),
        column_project,
        preferred_element_type=jnp.float32,
    ).astype(jnp.bfloat16)
    combined = combined.reshape(attend_seq_total, element_count, HEAD_NUMBER, 4, HEAD_BREADTH)
    scores = jnp.einsum(
        "snhd,tnhd->nhst",
        combined[:, :, :, 0],
        combined[:, :, :, 1],
        preferred_element_type=jnp.float32,
    ) / math.sqrt(HEAD_BREADTH)
    weights = jax.nn.softmax(scores, axis=-1).astype(jnp.bfloat16)
    mixture = jnp.einsum(
        "nhst,tnhd->snhd", weights, combined[:, :, :, 2], preferred_element_type=jnp.float32
    )
    gated = (jax.nn.sigmoid(combined[:, :, :, 3].astype(jnp.float32)) * mixture).astype(
        jnp.bfloat16
    )
    renewed = column_list.astype(jnp.float32) + jnp.dot(
        gated.reshape(attend_seq_total, element_count, HEAD_NUMBER * HEAD_BREADTH),
        vertical_projector,
        preferred_element_type=jnp.float32,
    )
    outer_ab = jnp.dot(
        normalized_state(renewed).astype(jnp.bfloat16),
        tensor_pair_maps,
        preferred_element_type=jnp.float32,
    ).astype(jnp.bfloat16)
    renewed_rows = renewed.astype(jnp.bfloat16).reshape(
        attend_seq_total, 1, 1, element_count, alignment_width
    )
    returned = lax.all_to_all(renewed_rows, "row", split_axis=0, concat_axis=1, tiled=True)
    revised_homolog_matrix, outer_ab = (
        returned,
        outer_ab.reshape(attend_seq_total, 1, 1, element_count, 2 * OUTER_CHANNELS),
    )
    seq_total = outer_ab.shape[0]
    left_rows = lax.all_gather(outer_ab[..., :OUTER_CHANNELS], "col", axis=2, tiled=True).reshape(
        seq_total, pair_rows, OUTER_CHANNELS
    )
    segment_list = lax.all_gather(outer_ab[..., OUTER_CHANNELS:], "row", axis=1, tiled=True)
    piece_len = segment_list.shape[1]
    right_rows = segment_list.reshape(seq_total, piece_len * block_length, OUTER_CHANNELS)
    outer_prod = (
        jnp.einsum("sip,sjq->ijpq", left_rows, right_rows, preferred_element_type=jnp.float32)
        / seq_total
    )
    outer_prod = outer_prod.astype(jnp.bfloat16).reshape(
        pair_rows, piece_len * block_length, OUTER_CHANNELS * OUTER_CHANNELS
    )
    outer_terms = jnp.dot(outer_prod, outer_output, preferred_element_type=jnp.float32)
    outer_terms = outer_terms.reshape(pair_rows, piece_len, 1, block_length, pair_width)
    after_outer = pairs.astype(jnp.float32) + outer_terms

    def triangle(current, project, output, outgoing):
        flat_state = current.reshape(pair_rows, local_columns, pair_width)
        normed_state = normalized_state(flat_state).astype(jnp.bfloat16)
        channels = jnp.einsum(
            "rjz,zc->crj", normed_state, project[:, : 4 * C_TRI], preferred_element_type=jnp.float32
        )
        left_plane = (jax.nn.sigmoid(channels[:C_TRI]) * channels[C_TRI : 2 * C_TRI]).astype(
            jnp.bfloat16
        )
        right_plane = (
            jax.nn.sigmoid(channels[2 * C_TRI : 3 * C_TRI]) * channels[3 * C_TRI :]
        ).astype(jnp.bfloat16)
        gating = jax.nn.sigmoid(
            jnp.dot(normed_state, project[:, 4 * C_TRI :], preferred_element_type=jnp.float32)
        )
        left_chan, right_chan = (
            lax.all_to_all(left_plane, "row", split_axis=0, concat_axis=1, tiled=True),
            lax.all_to_all(right_plane, "row", split_axis=0, concat_axis=1, tiled=True),
        )
        local_channels = left_chan.shape[0]
        if outgoing:
            swapped = lax.all_to_all(
                right_chan.reshape(
                    local_channels, count_of_rows, col_count, block_length, 1, local_columns
                ),
                "col",
                split_axis=2,
                concat_axis=4,
                tiled=True,
            )
            swapped = swapped.reshape(local_channels, local_columns, col_count, local_columns)
            segment_list = lax.all_gather(
                left_chan.reshape(local_channels, 1, residues, local_columns),
                "col",
                axis=1,
                tiled=True,
            )
            joined = jnp.einsum(
                "lcim,ljcm->lij", segment_list, swapped, preferred_element_type=jnp.float32
            )
            mixture = joined.astype(jnp.bfloat16)
        else:
            mapped = jnp.einsum(
                "lckm,lkj->lcmj",
                lax.all_gather(
                    left_chan.reshape(local_channels, 1, residues, local_columns),
                    "col",
                    axis=1,
                    tiled=True,
                ),
                right_chan,
                preferred_element_type=jnp.float32,
            )
            mixture = mapped.astype(jnp.bfloat16).reshape(
                local_channels, col_count, count_of_rows, block_length, local_columns
            )
            mixture = mixture.transpose(0, 2, 1, 3, 4).reshape(
                local_channels, residues, local_columns
            )
        returned = lax.all_to_all(mixture, "row", split_axis=1, concat_axis=0, tiled=True)
        normed_mix = normalized_state(returned, 0).astype(jnp.bfloat16)
        state_increment = jnp.einsum(
            "crj,cz->rjz", normed_mix, output, preferred_element_type=jnp.float32
        )
        return current + (gating * state_increment).reshape(current.shape)

    after_out = triangle(after_outer, outgoing_project, outgoing_output, True)
    new_pairs = triangle(after_out, incoming_project, incoming_output, False)
    return (revised_homolog_matrix, new_pairs)


def solution(mesh):
    return jax.shard_map(
        shards,
        mesh=mesh,
        in_specs=(
            P("row", None, "col", None, None),
            P("row", None, "col", None, None),
            P(),
            P(),
            P(),
            P(),
            P(),
            P(),
            P(),
            P(),
            P(),
            P(),
            P(),
        ),
        out_specs=(P("row", None, "col", None, None), P("row", None, "col", None, None)),
        check_vma=False,
    )
```

profile of v0, /device:TPU:1, one launch (start us, length us, event | category | flops | bytes accessed | tf_op | source)
XLA Modules:
  0.0 700.8 jit_solution(8845954735496438248)
XLA Ops:
  10.0 15.6 %all-to-all-start.1 = ((bf16[8,4,128,1,1]{2,1,4,3,0:T(4,128)(2,1)}), bf16[8,4,128,1,1]{2,1,4,3,0:T(4,128)(2,1)S(1)}, u32[]{:S(2)}, u32[]{:S(2)}) async-start(bf16[8,4,128,1,1]{2,1,4,3,0:T(4,128)(2,1)} %copy.142), calls=%async_computation.1 | async-start | bytes 16384 | tf_op jit(solution)/shard_map/all_to_all | solution.py:60
  26.7 10.4 %all-to-all-done.1 = bf16[8,4,128,1,1]{2,1,4,3,0:T(4,128)(2,1)S(1)} async-done(((bf16[8,4,128,1,1]{2,1,4,3,0:T(4,128)(2,1)}), bf16[8,4,128,1,1]{2,1,4,3,0:T(4,128)(2,1)S(1)}, u32[]{:S(2)}, u32[]{:S(2)}) %all-to-all-start.1) | async-done | bytes 8224 | tf_op jit(solution)/shard_map/all_to_all | solution.py:60
  44.6 21.6 %all-to-all-done = bf16[2,128,1,1,8,128]{5,1,0,3,2,4:T(8,128)(2,1)S(1)} async-done(((bf16[2,128,1,1,8,128]{5,1,0,3,2,4:T(8,128)(2,1)}), bf16[2,128,1,1,8,128]{5,1,0,3,2,4:T(8,128)(2,1)S(1)}, u32[]{:S(2)}, u32[]{:S(2)}) %all-to-all-start) | async-done | bytes 524320 | tf_op jit(solution)/shard_map/all_to_all | solution.py:72
  69.2 163.5 %all-gather.6.cloned.1.call-done = bf16[2,512,128,4,1,1]{2,3,5,4,0,1:T(4,128)(2,1)} async-done(((bf16[2,4,128,4,1,1]{2,3,5,4,0,1:T(4,128)(2,1)}), bf16[2,512,128,4,1,1]{2,3,5,4,0,1:T(4,128)(2,1)}) %all-gather.6.cloned.1.call-update) | async-done | bytes 1048592 | tf_op jit(solution)/shard_map/all_gather | solution.py:61
  241.0 27.8 %all_to_all.126 = bf16[2,128,4,1,64]{1,4,3,0,2:T(8,128)(2,1)S(1)} all-to-all(bf16[2,128,4,1,64]{1,4,3,0,2:T(8,128)(2,1)S(1)} %copy.148), channel_id=1, replica_groups=mesh['row'=128,'col'=4] {'col'}, dimensions={2} | all-to-all | bytes 262144 | tf_op jit(solution)/shard_map/all_to_all | solution.py:97
  269.2 21.4 %all_to_all.127 = bf16[2,128,1,1,256]{4,0,3,2,1:T(2,128)(2,1)S(1)} all-to-all(bf16[2,128,1,1,256]{4,0,3,2,1:T(2,128)(2,1)S(1)} %copy.151), channel_id=1, replica_groups=mesh['row'=128,'col'=4] {'row'}, dimensions={1} | all-to-all | bytes 262144 | tf_op jit(solution)/shard_map/all_to_all | solution.py:109
  299.2 14.5 %all_gather.17 = bf16[256,1,4,1,32]{0,4,3,1,2:T(8,128)(2,1)S(1)} all-gather(bf16[256,1,1,1,32]{0,4,3,1,2:T(8,128)(2,1)S(1)} %get-tuple-element.59), channel_id=1, replica_groups=mesh['row'=128,'col'=4] {'col'}, dimensions={2}, use_global_device_ids=true | all-gather | bytes 81920 | tf_op jit(solution)/shard_map/all_gather | solution.py:151
  313.7 176.0 %all-gather.4.cloned.1.call-done = bf16[256,128,1,1,32]{0,4,3,2,1:T(8,128)(2,1)} async-done(((bf16[256,1,1,1,32]{0,4,3,2,1:T(8,128)(2,1)}), bf16[256,128,1,1,32]{0,4,3,2,1:T(8,128)(2,1)}) %all-gather.4.cloned.1.call-update) | async-done | bytes 2097168 | tf_op jit(solution)/shard_map/all_gather | solution.py:154
  496.1 8.5 %all-to-all-start.6 = ((bf16[128,4,128]{2,1,0:T(4,128)(2,1)}), bf16[128,4,128]{2,1,0:T(4,128)(2,1)S(1)}, u32[]{:S(2)}, u32[]{:S(2)}) async-start(bf16[128,4,128]{2,1,0:T(4,128)(2,1)} %copy.172), calls=%async_computation.6 | async-start | bytes 262144 | tf_op jit(solution)/shard_map/all_to_all | solution.py:185
  505.4 10.0 %all-to-all-done.6 = bf16[128,4,128]{2,1,0:T(4,128)(2,1)S(1)} async-done(((bf16[128,4,128]{2,1,0:T(4,128)(2,1)}), bf16[128,4,128]{2,1,0:T(4,128)(2,1)S(1)}, u32[]{:S(2)}, u32[]{:S(2)}) %all-to-all-start.6) | async-done | bytes 131104 | tf_op jit(solution)/shard_map/all_to_all | solution.py:185
  515.4 6.1 all-to-all-start.5
  522.2 10.0 %all-to-all-done.5 = bf16[128,4,128]{2,1,0:T(4,128)(2,1)S(1)} async-done(((bf16[128,4,128]{2,1,0:T(4,128)(2,1)}), bf16[128,4,128]{2,1,0:T(4,128)(2,1)S(1)}, u32[]{:S(2)}, u32[]{:S(2)}) %all-to-all-start.5) | async-done | bytes 131104 | tf_op jit(solution)/shard_map/all_to_all | solution.py:184
  532.2 10.4 %all-to-all-start.7 = ((bf16[1,128,4,1,1,128]{1,5,4,3,0,2:T(8,128)(2,1)}), bf16[1,128,4,1,1,128]{1,5,4,3,0,2:T(8,128)(2,1)S(1)}, u32[]{:S(2)}, u32[]{:S(2)}) async-start(bf16[1,128,4,1,1,128]{1,5,4,3,0,2:T(8,128)(2,1)} %copy.173), calls=%async_computation.7 | async-start | bytes 262144 | tf_op jit(solution)/shard_map/all_to_all | solution.py:189
  542.6 30.4 %all_gather.18 = bf16[1,4,512,128]{3,2,0,1:T(8,128)(2,1)S(1)} all-gather(bf16[1,1,512,128]{3,2,0,1:T(8,128)(2,1)S(1)} %bitcast.327), channel_id=1, replica_groups=mesh['row'=128,'col'=4] {'col'}, dimensions={1}, use_global_device_ids=true | all-gather | bytes 655360 | tf_op jit(solution)/shard_map/all_gather | solution.py:199
  576.4 8.3 %all-to-all-start.8 = ((bf16[128,2,256]{2,1,0:T(2,128)(2,1)}), bf16[128,2,256]{2,1,0:T(2,128)(2,1)S(1)}, u32[]{:S(2)}, u32[]{:S(2)}) async-start(bf16[128,2,256]{2,1,0:T(2,128)(2,1)} %reshape.493), calls=%async_computation.8 | async-start | bytes 262144 | tf_op jit(solution)/shard_map/all_to_all | solution.py:227
  585.0 10.5 %all-to-all-done.8 = bf16[128,2,256]{2,1,0:T(2,128)(2,1)S(1)} async-done(((bf16[128,2,256]{2,1,0:T(2,128)(2,1)}), bf16[128,2,256]{2,1,0:T(2,128)(2,1)S(1)}, u32[]{:S(2)}, u32[]{:S(2)}) %all-to-all-start.8) | async-done | bytes 131104 | tf_op jit(solution)/shard_map/all_to_all | solution.py:227
  597.7 6.1 all-to-all-start.9
  604.5 10.0 %all-to-all-done.9 = bf16[128,4,128]{2,1,0:T(4,128)(2,1)S(1)} async-done(((bf16[128,4,128]{2,1,0:T(4,128)(2,1)}), bf16[128,4,128]{2,1,0:T(4,128)(2,1)S(1)}, u32[]{:S(2)}, u32[]{:S(2)}) %all-to-all-start.9) | async-done | bytes 131104 | tf_op jit(solution)/shard_map/all_to_all | solution.py:184
  614.5 6.1 all-to-all-start.10
  622.1 9.2 %all-to-all-done.10 = bf16[128,4,128]{2,1,0:T(4,128)(2,1)S(1)} async-done(((bf16[128,4,128]{2,1,0:T(4,128)(2,1)}), bf16[128,4,128]{2,1,0:T(4,128)(2,1)S(1)}, u32[]{:S(2)}, u32[]{:S(2)}) %all-to-all-start.10) | async-done | bytes 131104 | tf_op jit(solution)/shard_map/all_to_all | solution.py:185
  631.3 6.1 all-to-all-start.4
  637.4 21.7 %all_gather.19 = bf16[1,4,512,128]{3,2,0,1:T(8,128)(2,1)S(1)} all-gather(bf16[1,1,512,128]{3,2,0,1:T(8,128)(2,1)S(1)} %bitcast.326), channel_id=1, replica_groups=mesh['row'=128,'col'=4] {'col'}, dimensions={1}, use_global_device_ids=true | all-gather | bytes 655360 | tf_op jit(solution)/shard_map/all_gather | solution.py:212
  662.0 19.6 %all-to-all-start.11 = ((bf16[128,2,256]{2,1,0:T(2,128)(2,1)}), bf16[128,2,256]{2,1,0:T(2,128)(2,1)S(1)}, u32[]{:S(2)}, u32[]{:S(2)}) async-start(bf16[128,2,256]{2,1,0:T(2,128)(2,1)} %reshape.495), calls=%async_computation.11 | async-start | bytes 262144 | tf_op jit(solution)/shard_map/all_to_all | solution.py:227
  683.5 8.9 %all-to-all-done.11 = bf16[128,2,256]{2,1,0:T(2,128)(2,1)S(1)} async-done(((bf16[128,2,256]{2,1,0:T(2,128)(2,1)}), bf16[128,2,256]{2,1,0:T(2,128)(2,1)S(1)}, u32[]{:S(2)}, u32[]{:S(2)}) %all-to-all-start.11) | async-done | bytes 131104 | tf_op jit(solution)/shard_map/all_to_all | solution.py:227
  (140 shorter events, 57.5 us)
Async XLA Ops:
  7.2 31.6 %copy-start = (bf16[256,1024]{1,0:T(8,128)(2,1)S(1)}, bf16[256,1024]{1,0:T(8,128)(2,1)}, u32[]{:S(2)}) copy-start(bf16[256,1024]{1,0:T(8,128)(2,1)} %param.17) | copy-start | bytes 1572868
  10.0 27.0 %all-to-all-start.1 = ((bf16[8,4,128,1,1]{2,1,4,3,0:T(4,128)(2,1)}), bf16[8,4,128,1,1]{2,1,4,3,0:T(4,128)(2,1)S(1)}, u32[]{:S(2)}, u32[]{:S(2)}) async-start(bf16[8,4,128,1,1]{2,1,4,3,0:T(4,128)(2,1)} %copy.142), calls=%async_computation.1 | async-start | bytes 16384 | tf_op jit(solution)/shard_map/all_to_all | solution.py:60
  25.6 207.1 %all-gather.6.cloned.1.call-start = ((), (), s32[]{:S(2)}) async-start(), calls=%async_computation.13 | async-start | bytes 1056768 | tf_op jit(solution)/shard_map/all_gather | solution.py:61
  41.1 25.2 %all-to-all-start = ((bf16[2,128,1,1,8,128]{5,1,0,3,2,4:T(8,128)(2,1)}), bf16[2,128,1,1,8,128]{5,1,0,3,2,4:T(8,128)(2,1)S(1)}, u32[]{:S(2)}, u32[]{:S(2)}) async-start(bf16[2,128,1,1,8,128]{5,1,0,3,2,4:T(8,128)(2,1)} %copy.138), calls=%async_computation | async-start | bytes 1048576 | tf_op jit(solution)/shard_map/all_to_all | solution.py:72
  44.5 445.2 %all-gather.4.cloned.1.call-start = ((), (), s32[]{:S(2)}) async-start(), calls=%async_computation.12 | async-start | bytes 2113536 | tf_op jit(solution)/shard_map/all_gather | solution.py:154
  240.1 28.7 %copy-start.1 = (bf16[2,128,1,1,256]{4,1,3,2,0:T(8,128)(2,1)S(1)}, bf16[2,128,1,1,256]{4,1,3,2,0:T(8,128)(2,1)}, u32[]{:S(2)}) copy-start(bf16[2,128,1,1,256]{4,1,3,2,0:T(8,128)(2,1)} %param.15) | copy-start | bytes 393220
  240.1 28.7 %copy-start.4 = (bf16[256,256]{1,0:T(8,128)(2,1)S(1)}, bf16[256,256]{1,0:T(8,128)(2,1)}, u32[]{:S(2)}) copy-start(bf16[256,256]{1,0:T(8,128)(2,1)} %param.18) | copy-start | bytes 393220
  268.8 26.8 %copy-start.2 = (bf16[256,1024]{1,0:T(8,128)(2,1)S(1)}, bf16[256,1024]{1,0:T(8,128)(2,1)}, u32[]{:S(2)}) copy-start(bf16[256,1024]{1,0:T(8,128)(2,1)} %param.20) | copy-start | bytes 1572868
  297.0 1.1 copy-start.5
  297.0 1.4 copy-start.8
  493.2 1.2 copy-start.3
  493.7 1.1 copy-start.6
  496.1 19.3 %all-to-all-start.6 = ((bf16[128,4,128]{2,1,0:T(4,128)(2,1)}), bf16[128,4,128]{2,1,0:T(4,128)(2,1)S(1)}, u32[]{:S(2)}, u32[]{:S(2)}) async-start(bf16[128,4,128]{2,1,0:T(4,128)(2,1)} %copy.172), calls=%async_computation.6 | async-start | bytes 262144 | tf_op jit(solution)/shard_map/all_to_all | solution.py:185
  515.4 16.8 %all-to-all-start.5 = ((bf16[128,4,128]{2,1,0:T(4,128)(2,1)}), bf16[128,4,128]{2,1,0:T(4,128)(2,1)S(1)}, u32[]{:S(2)}, u32[]{:S(2)}) async-start(bf16[128,4,128]{2,1,0:T(4,128)(2,1)} %copy.170), calls=%async_computation.5 | async-start | bytes 262144 | tf_op jit(solution)/shard_map/all_to_all | solution.py:184
  532.2 40.9 %all-to-all-start.7 = ((bf16[1,128,4,1,1,128]{1,5,4,3,0,2:T(8,128)(2,1)}), bf16[1,128,4,1,1,128]{1,5,4,3,0,2:T(8,128)(2,1)S(1)}, u32[]{:S(2)}, u32[]{:S(2)}) async-start(bf16[1,128,4,1,1,128]{1,5,4,3,0,2:T(8,128)(2,1)} %copy.173), calls=%async_computation.7 | async-start | bytes 262144 | tf_op jit(solution)/shard_map/all_to_all | solution.py:189
  573.4 22.7 %copy-start.9 = (bf16[128,128]{1,0:T(8,128)(2,1)S(1)}, bf16[128,128]{1,0:T(8,128)(2,1)}, u32[]{:S(2)}) copy-start(bf16[128,128]{1,0:T(8,128)(2,1)} %param.25) | copy-start | bytes 98308
  576.4 20.0 %copy-start.7 = (bf16[128,640]{1,0:T(8,128)(2,1)S(1)}, bf16[128,640]{1,0:T(8,128)(2,1)}, u32[]{:S(2)}) copy-start(bf16[128,640]{1,0:T(8,128)(2,1)} %param.26) | copy-start | bytes 491524
  576.4 19.1 %all-to-all-start.8 = ((bf16[128,2,256]{2,1,0:T(2,128)(2,1)}), bf16[128,2,256]{2,1,0:T(2,128)(2,1)S(1)}, u32[]{:S(2)}, u32[]{:S(2)}) async-start(bf16[128,2,256]{2,1,0:T(2,128)(2,1)} %reshape.493), calls=%async_computation.8 | async-start | bytes 262144 | tf_op jit(solution)/shard_map/all_to_all | solution.py:227
  597.7 16.8 %all-to-all-start.9 = ((bf16[128,4,128]{2,1,0:T(4,128)(2,1)}), bf16[128,4,128]{2,1,0:T(4,128)(2,1)S(1)}, u32[]{:S(2)}, u32[]{:S(2)}) async-start(bf16[128,4,128]{2,1,0:T(4,128)(2,1)} %copy.181), calls=%async_computation.9 | async-start | bytes 262144 | tf_op jit(solution)/shard_map/all_to_all | solution.py:184
  614.5 16.8 %all-to-all-start.10 = ((bf16[128,4,128]{2,1,0:T(4,128)(2,1)}), bf16[128,4,128]{2,1,0:T(4,128)(2,1)S(1)}, u32[]{:S(2)}, u32[]{:S(2)}) async-start(bf16[128,4,128]{2,1,0:T(4,128)(2,1)} %copy.184), calls=%async_computation.10 | async-start | bytes 262144 | tf_op jit(solution)/shard_map/all_to_all | solution.py:185
  631.3 30.6 %all-to-all-start.4 = ((bf16[128,2,256]{2,1,0:T(2,128)(2,1)}), bf16[128,2,256]{2,1,0:T(2,128)(2,1)S(1)}, u32[]{:S(2)}, u32[]{:S(2)}) async-start(bf16[128,2,256]{2,1,0:T(2,128)(2,1)} %reshape.491), calls=%async_computation.4 | async-start | bytes 262144 | tf_op jit(solution)/shard_map/all_to_all | solution.py:145
  662.0 30.9 %copy-start.10 = (bf16[128,128]{1,0:T(8,128)(2,1)S(1)}, bf16[128,128]{1,0:T(8,128)(2,1)}, u32[]{:S(2)}) copy-start(bf16[128,128]{1,0:T(8,128)(2,1)} %param.27) | copy-start | bytes 98308
  662.0 30.4 %all-to-all-start.11 = ((bf16[128,2,256]{2,1,0:T(2,128)(2,1)}), bf16[128,2,256]{2,1,0:T(2,128)(2,1)S(1)}, u32[]{:S(2)}, u32[]{:S(2)}) async-start(bf16[128,2,256]{2,1,0:T(2,128)(2,1)} %reshape.495), calls=%async_computation.11 | async-start | bytes 262144 | tf_op jit(solution)/shard_map/all_to_all | solution.py:227
Sparse Core Ops, SparseCore 0:
  37.8 194.8 all-gather.5
  299.3 190.3 all-gather.3
where the time goes:
time: 702 us; the launch traced here: 701 us
  waiting for transfers between devices  430 us (61%)
  blocking collectives  116 us (17%)
  starting transfers between devices  90.3 us (13%)
  local copies, waits for them, and re-layouts  26.1 us (4%)
  between operations  14.7 us (2%)
  matrix products  12 us (2%)
  other arithmetic  11.8 us (2%)
    all_gather x1, waiting for transfers between devices, shards(): lax.all_gather(outer_ab[..., OUTER_CHANNELS:], 'row', axis=1, tiled=True)  176 us
    all_gather x1, waiting for transfers between devices, shards(): full_bias = lax.all_gather(spread_bias, 'row', axis=1, tiled=True)  164 us
    all_gather x2, blocking collectives, triangle(): lax.all_gather(left_chan.reshape(local_channels, 1, residues, local_colum...  52.1 us
    all_to_all x2, starting transfers between devices, triangle(): lax.all_to_all(mixture, 'row', split_axis=1, concat_axis=0, tiled=True)  28 us
    all_to_all x1, blocking collectives, shards(): lax.all_to_all(shortened(gated), 'col', split_axis=2, concat_axis=4, tile...  27.8 us
    all_to_all x1, waiting for transfers between devices, shards(): lax.all_to_all(projected, 'col', split_axis=4, concat_axis=2, tiled=True)  21.6 us
    all_to_all x1, blocking collectives, shards(): lax.all_to_all(state_after_rows, 'row', split_axis=1, concat_axis=0, tile...  21.4 us
    all_to_all x2, waiting for transfers between devices, triangle(): lax.all_to_all(left_plane, 'row', split_axis=0, concat_axis=1, tiled=True)  19.9 us
  transfers between devices with their start and end apart: 12, of which 10 were waited for; matrix products, arithmetic and copies ran while one was open for 2% of the time, Pallas kernels for 0%

commit v1 on v0

v1 whole, which is shorter than its diff:
```python
import functools
import math

import jax
import jax.numpy as jnp
from jax import lax
from jax.experimental import pallas as pl
from jax.experimental.pallas import tpu as pltpu
from jax.sharding import PartitionSpec as P

MESH = pl.DeviceIdType.MESH
BF = jnp.bfloat16
F32 = jnp.float32
EPS = 1e-05
HEADS = 8
NXY = 16
NZC = 8
NCOL = 4


def nn(a, b):
    return lax.dot_general(a, b, (((1,), (0,)), ((), ())), preferred_element_type=F32)


def nt(a, b):
    return lax.dot_general(a, b, (((1,), (1,)), ((), ())), preferred_element_type=F32)


def tn(a, b):
    return lax.dot_general(a, b, (((0,), (0,)), ((), ())), preferred_element_type=F32)


def norm(x, axis=-1):
    c = x - jnp.mean(x, axis=axis, keepdims=True)
    v = jnp.mean(c * c, axis=axis, keepdims=True)
    return c * lax.rsqrt(v + EPS)


def sig(x):
    return 1.0 / (1.0 + jnp.exp(-x))


def perm(sizes, order):
    n = math.prod(sizes)
    strides = [math.prod(sizes[k + 1 :]) for k in range(len(sizes))]
    out = lax.broadcasted_iota(jnp.int32, (n, n), 0)
    src = jnp.zeros((n, n), jnp.int32)
    rest = out
    for axis in reversed(order):
        src = src + (rest & (sizes[axis] - 1)) * strides[axis]
        rest = lax.shift_right_logical(rest, int(math.log2(sizes[axis])))
    inp = lax.broadcasted_iota(jnp.int32, (n, n), 1)
    return jnp.where(src == inp, 1.0, 0.0).astype(BF)


def where_am_i():
    row, col = lax.axis_index("row"), lax.axis_index("col")
    return row, col, row // NZC, row % NZC


class Swap:
    def __init__(self, r, name):
        self.send, self.recv = r[name + "_s"], r[name + "_r"]
        self.row, self.col, self.xy, self.zc = where_am_i()

    def put(self, src, dst, row, col):
        pltpu.make_async_remote_copy(
            src_ref=src,
            dst_ref=dst,
            send_sem=self.send,
            recv_sem=self.recv,
            device_id=(row, col),
            device_id_type=MESH,
        ).start()

    def keep(self, src, dst):
        pltpu.make_async_copy(src, dst, self.recv).start()

    def peers(self, kind):
        if kind == "xy":
            for d in range(1, NXY):
                g = lax.rem(self.xy + d, NXY)
                yield g, g * NZC + self.zc, self.col
        elif kind == "zc":
            for d in range(1, NZC):
                g = lax.rem(self.zc + d, NZC)
                yield g, self.xy * NZC + g, self.col
        else:
            for d in range(1, NCOL):
                g = lax.rem(self.col + d, NCOL)
                yield g, self.row, g

    def mine(self, kind):
        return {"xy": self.xy, "zc": self.zc, "col": self.col}[kind]

    def exchange(self, kind, src, dst):
        me = self.mine(kind)
        for g, row, col in self.peers(kind):
            self.put(src.at[g], dst.at[me], row, col)
        self.keep(src.at[me], dst.at[me])

    def gather(self, kind, buf):
        me = self.mine(kind)
        for g, row, col in self.peers(kind):
            self.put(buf.at[me], buf.at[me], row, col)

    def got(self, ref):
        pltpu.make_async_copy(ref, ref, self.recv).wait()

    def sent(self, ref):
        pltpu.make_async_copy(ref, ref, self.send).wait()


def barrier_signal():
    row, col, xy, zc = where_am_i()
    sem = pltpu.get_barrier_semaphore()

    def hail(r, c):
        pl.semaphore_signal(sem, inc=1, device_id=(r, c), device_id_type=MESH)

    for d in range(1, NXY):
        hail(lax.rem(xy + d, NXY) * NZC + zc, col)
    for d in range(1, NZC):
        hail(xy * NZC + lax.rem(zc + d, NZC), col)
    for d in range(1, NCOL):
        hail(row, lax.rem(col + d, NCOL))


def barrier_wait():
    pl.semaphore_wait(pltpu.get_barrier_semaphore(), NXY + NZC + NCOL - 3)


def attend(keys, own, weights, bias):
    length = keys.shape[0]
    q = nn(own, weights[:, 0:256]).astype(BF)
    k = nn(keys, weights[:, 256:512]).astype(BF)
    v = nn(keys, weights[:, 512:768]).astype(BF)
    gate = nn(own, weights[:, 768:1024]).astype(BF).astype(F32)
    v = jnp.concatenate([v, jnp.ones((length, 128), BF)], axis=1)
    head = lax.broadcasted_iota(jnp.int32, q.shape, 1) // 32
    total = jnp.zeros(q.shape, F32)
    for h in range(HEADS):
        scores = nt(jnp.where(head == h, q, jnp.zeros_like(q)), k) * (1.0 / math.sqrt(32.0))
        if bias is not None:
            scores = scores + bias(h)
        top = jnp.max(scores, axis=-1, keepdims=True)
        p = jnp.exp(scores - top).astype(BF)
        mixed = nn(p, v)
        inv = 1.0 / mixed[:, 256:384]
        mixed = mixed[:, 0:256] * jnp.concatenate([inv, inv], axis=1)
        total = total + jnp.where(head == h, mixed, 0.0)
    return (sig(gate) * total).astype(BF)


def by_kind(ref):
    w = ref[...]
    return jnp.concatenate(
        [w[:, 128 * h + 32 * k : 128 * h + 32 * k + 32] for k in range(4) for h in range(HEADS)], axis=1
    )


ROW_SCRATCH = dict(
    xg=((2, 4, 128, 256), BF),
    bsend=((4, 8, 128), F32),
    brecv=((4, 8, 128), F32),
    bz=((8, 16, 256), BF),
    bx=((16, 128, 256), BF),
    wrow=((256, 1024), BF),
)
ROW_SEMS = ["m0", "m1", "b0", "b1", "b2"]


def row_part(r):
    row, col, xy, zc = where_am_i()
    m = r["msa"]
    x = norm(m[...].astype(F32)).astype(BF)
    xg = r["xg"]
    for s in range(2):
        xg[s, col] = x[s]
    barrier_wait()
    swaps = [Swap(r, "m0"), Swap(r, "m1")]
    zn = norm(r["pairs"][...].astype(F32)).astype(BF).reshape(512, 128)
    bias_t = nt(r["pair_bias"][...].T, zn)
    for k in range(4):
        r["bsend"][k] = bias_t[:, 128 * k : 128 * k + 128]
    s0 = Swap(r, "b0")
    s0.exchange("col", r["bsend"], r["brecv"])
    for s in range(2):
        swaps[s].gather("col", xg.at[s])
    r["wrow"][...] = by_kind(r["row_w"])
    s0.got(r["brecv"])
    b = r["brecv"]
    lo = jnp.concatenate([b[0], b[1]], axis=1)
    hi = jnp.concatenate([b[2], b[3]], axis=1)
    r["bz"][zc] = jnp.concatenate([lo, hi], axis=0).astype(BF)
    s1 = Swap(r, "b1")
    s1.gather("zc", r["bz"])
    pz = perm((8, 16), (1, 0))
    s1.got(r["bz"].at[pl.ds(0, 7)])
    r["bx"][xy] = nn(pz, r["bz"][...].reshape(128, 256)).astype(BF)
    s2 = Swap(r, "b2")
    s2.gather("xy", r["bx"])
    if "prep" in r:
        r["prep"]()
    s2.got(r["bx"].at[pl.ds(0, 15)])
    cache = {}

    def bias(h):
        if h not in cache:
            pair = h // 2 * 2
            parts = []
            for jh in range(2):
                at = (jh * 8 + pair) * 8
                parts.append(r["bx"][:, at : at + 16, :].astype(F32))
            for k in range(2):
                cache[pair + k] = jnp.concatenate(
                    [p[:, 8 * k : 8 * k + 8].reshape(128, 256) for p in parts], axis=1
                )
        return cache[h]

    for s in range(2):
        swaps[s].got(xg.at[s, pl.ds(0, 3)])
        cache.clear()
        gated = attend(xg[s].reshape(512, 256), xg[s, col], r["wrow"], bias)
        r["m1"][s] = (m[s].astype(F32) + nn(gated, r["row_out"][...])).astype(BF)
    for s in range(2):
        swaps[s].sent(xg.at[s, pl.ds(0, 3)])
    s0.sent(r["bsend"].at[pl.ds(0, 3)])
    s1.sent(r["bz"].at[pl.ds(0, 7)])
    s2.sent(r["bx"].at[pl.ds(0, 15)])


COL_SCRATCH = dict(
    cs1=((16, 16, 256), BF),
    cr1=((16, 16, 256), BF),
    cs2=((8, 32, 256), BF),
    cr2=((8, 32, 256), BF),
    ds1=((8, 32, 256), BF),
    dr1=((8, 32, 256), BF),
    ds2=((16, 16, 256), BF),
    dr2=((16, 16, 256), BF),
    lg=((4, 32, 256), BF),
    rz=((8, 32, 256), BF),
    rx=((16, 256, 256), BF),
    wcol=((256, 1024), BF),
    bd=((32, 128, 512), BF),
)
COL_SEMS = ["c1", "c2", "d1", "d2", "lg", "rz", "rx", "rc"]


def col_prep(r):
    r["wcol"][...] = by_kind(r["col_w"])
    by_u = nn(perm((32, 32), (1, 0)), r["outer_out"][...]).astype(BF).reshape(32, 32, 128)
    r["bd"][...] = jnp.zeros((32, 128, 512), BF)
    for i in range(4):
        r["bd"][:, 32 * i : 32 * i + 32, 128 * i : 128 * i + 128] = by_u


def col_part(r):
    row, col, xy, zc = where_am_i()
    core = lax.rem(zc, 2)
    m1 = r["m1"][...].astype(F32).reshape(2, 16, 8, 256)
    r["cs1"][...] = jnp.concatenate([m1[0], m1[1]], axis=1).astype(BF)
    c1 = Swap(r, "c1")
    c1.exchange("xy", r["cs1"], r["cr1"])
    to_zc = perm((16, 2, 8), (2, 0, 1))
    c1.got(r["cr1"])
    r["cs2"][...] = nn(to_zc, r["cr1"][...].reshape(256, 256)).astype(BF).reshape(8, 32, 256)
    c2 = Swap(r, "c2")
    c2.exchange("zc", r["cs2"], r["cr2"])
    c2.got(r["cr2"])
    lines = r["cr2"][...].reshape(256, 256).astype(F32)
    x = norm(lines).astype(BF)
    gated = attend(x, x, r["wcol"], None)
    m2 = lines + nn(gated, r["col_out"][...])
    x = norm(m2).astype(BF)
    ab = nt(r["maps"][...].T, x).astype(BF)
    r["lg"][col] = ab[0:32]
    r["rz"][zc] = ab[32:64]
    rz = Swap(r, "rz")
    rz.gather("zc", r["rz"])
    lg = Swap(r, "lg")
    lg.gather("col", r["lg"])
    r["ds1"][...] = m2.astype(BF).reshape(8, 32, 256)
    d1 = Swap(r, "d1")
    d1.exchange("zc", r["ds1"], r["dr1"])
    rz.got(r["rz"].at[pl.ds(0, 7)])
    right = nn(perm((8, 32), (1, 0)), r["rz"][...].reshape(256, 256)).astype(BF)
    rx = r["rx"]
    for k in range(2):

        @pl.when(core == k)
        def _():
            rx[xy, 128 * k : 128 * k + 128] = right[128 * k : 128 * k + 128]

    half = pl.ds(pl.multiple_of(core * 128, 128), 128)
    other = pl.ds(pl.multiple_of(128 - core * 128, 128), 128)
    rxs = Swap(r, "rx")
    for g, prow, pcol in rxs.peers("xy"):
        rxs.put(rx.at[xy, half], rx.at[xy, half], prow, pcol)
    d1.got(r["dr1"])
    r["ds2"][...] = nn(perm((8, 16, 2), (1, 2, 0)), r["dr1"][...].reshape(256, 256)).astype(BF).reshape(16, 16, 256)
    d2 = Swap(r, "d2")
    d2.exchange("xy", r["ds2"], r["dr2"])
    lg.got(r["lg"].at[pl.ds(0, 3)])
    left = r["lg"][...].reshape(128, 256).T
    rxs.got(rx.at[pl.ds(0, 15), pl.ds(0, 128)])
    rc = Swap(r, "rc")
    rc.put(rx.at[:, half], rx.at[:, half], row + 1 - 2 * core, col)
    d2.got(r["dr2"])
    dr2 = r["dr2"][...].astype(F32)
    for s in range(2):
        r["msa_out"][s] = dr2[:, 8 * s : 8 * s + 8].reshape(128, 256).astype(BF)

    def add(base, acc):
        for up in range(8):
            at = pl.multiple_of(base * 8 + up * 16, 16)
            block = rx[:, pl.ds(at, 16), :].astype(F32)
            for k in range(2):
                a = nn(left, r["bd"][base + 2 * up + k]).astype(BF)
                acc = acc + nn(block[:, 8 * k : 8 * k + 8].reshape(128, 256).astype(BF), a)
        return acc

    acc = add(core * 16, jnp.zeros((128, 512), F32))
    rc.got(rx.at[:, other])
    acc = add(16 - core * 16, acc)
    for i in range(4):
        r["z1"][i] = r["pairs"][i].astype(F32) + acc[:, 128 * i : 128 * i + 128] * (1.0 / 256.0)
    c1.sent(r["cs1"].at[pl.ds(0, 15)])
    c2.sent(r["cs2"].at[pl.ds(0, 7)])
    d1.sent(r["ds1"].at[pl.ds(0, 7)])
    d2.sent(r["ds2"].at[pl.ds(0, 15)])
    lg.sent(r["lg"].at[pl.ds(0, 3)])
    rz.sent(r["rz"].at[pl.ds(0, 7)])
    rxs.sent(rx.at[pl.ds(0, 15), pl.ds(0, 128)])
    rc.sent(rx.at[:, half])


def tri_scratch(t):
    return {
        t + "s1": ((16, 16, 512), BF),
        t + "r1": ((16, 16, 512), BF),
        t + "s2": ((8, 32, 512), BF),
        t + "r2": ((8, 32, 512), BF),
        t + "ps": ((4, 512, 128), BF),
        t + "pr": ((4, 512, 128), BF),
        t + "s3": ((16, 32, 128), BF),
        t + "r3": ((16, 32, 128), BF),
        t + "s4": ((8, 64, 128), BF),
        t + "r4": ((8, 64, 128), BF),
        t + "gate": ((512, 128), F32),
        t + "wg": ((256, 128), BF),
        t + "wv": ((256, 128), BF),
        t + "wo": ((128, 128), BF),
    }


def tri_sems(t):
    return [t + k for k in ("1", "2", "p", "3", "4")]


def tri_prep(r, t):
    w = r[t + "_proj"][:, 0:512].astype(F32).T.reshape(4, 16, 8, 128)
    r[t + "wg"][...] = jnp.concatenate([w[0], w[2]], axis=1).astype(BF).reshape(256, 128)
    r[t + "wv"][...] = jnp.concatenate([w[1], w[3]], axis=1).astype(BF).reshape(256, 128)
    r[t + "wo"][...] = nn(perm((16, 8), (1, 0)), r[t + "_out"][...]).astype(BF)


def tri_part(r, t, src, dst, outgoing):
    row, col, xy, zc = where_am_i()
    x = norm(r[src][...]).astype(BF).reshape(512, 128)
    both = sig(nt(r[t + "wg"][...], x)) * nt(r[t + "wv"][...], x)
    r[t + "s1"][...] = both.astype(BF).reshape(16, 16, 512)
    e1 = Swap(r, t + "1")
    e1.exchange("xy", r[t + "s1"], r[t + "r1"])
    r[t + "gate"][...] = sig(nn(x, r[t + "_proj"][:, 512:640]))
    to_zc = perm((16, 2, 8), (2, 1, 0))
    e1.got(r[t + "r1"])
    r[t + "s2"][...] = nn(to_zc, r[t + "r1"][...].reshape(256, 512)).astype(BF).reshape(8, 32, 512)
    e2 = Swap(r, t + "2")
    e2.exchange("zc", r[t + "s2"], r[t + "r2"])
    natural = perm((8, 16), (1, 0))
    e2.got(r[t + "r2"])
    left = r[t + "r2"][:, 0:16, :].reshape(128, 512)
    right = r[t + "r2"][:, 16:32, :].reshape(128, 512)
    ep = Swap(r, t + "p")
    if outgoing:
        left = nn(natural, left).astype(BF)
        right = nn(natural, right).astype(BF)
        left = jnp.concatenate([left[:, 128 * q : 128 * q + 128] for q in range(4)], axis=0)
        for q in range(4):
            r[t + "ps"][q] = nt(left, right[:, 128 * q : 128 * q + 128]).astype(BF)
        ep.exchange("col", r[t + "ps"], r[t + "pr"])
        ep.got(r[t + "pr"])
        pr = r[t + "pr"]
        mix = (pr[0].astype(F32) + pr[1].astype(F32)) + (pr[2].astype(F32) + pr[3].astype(F32))
    else:
        gathered = r[t + "pg"]
        gathered[col] = jnp.concatenate([left[:, 128 * q : 128 * q + 128].T for q in range(4)], axis=1)
        ep.gather("col", gathered)
        right = jnp.concatenate([right[:, 128 * q : 128 * q + 128] for q in range(4)], axis=0)
        ep.got(gathered.at[pl.ds(0, 3)])
        mix = nn(gathered[...].reshape(512, 512), right)
    mix = mix.reshape(4, 16, 8, 128)
    r[t + "s3"][...] = jnp.concatenate([mix[q] for q in range(4)], axis=1).astype(BF)
    e3 = Swap(r, t + "3")
    e3.exchange("xy", r[t + "s3"], r[t + "r3"])
    back = perm((16, 4, 8), (2, 1, 0))
    e3.got(r[t + "r3"])
    r[t + "s4"][...] = nn(back, r[t + "r3"][...].reshape(512, 128)).astype(BF).reshape(8, 64, 128)
    e4 = Swap(r, t + "4")
    e4.exchange("zc", r[t + "s4"], r[t + "r4"])
    e4.got(r[t + "r4"])
    for q in range(4):
        mq = r[t + "r4"][:, 16 * q : 16 * q + 16, :].reshape(128, 128).astype(F32)
        step = tn(norm(mq, 0).astype(BF), r[t + "wo"][...])
        r[dst][q] = r[src][q] + r[t + "gate"][128 * q : 128 * q + 128] * step
    e1.sent(r[t + "s1"].at[pl.ds(0, 15)])
    e2.sent(r[t + "s2"].at[pl.ds(0, 7)])
    if outgoing:
        ep.sent(r[t + "ps"].at[pl.ds(0, 3)])
    else:
        ep.sent(r[t + "pg"].at[pl.ds(0, 3)])
    e3.sent(r[t + "s3"].at[pl.ds(0, 15)])
    e4.sent(r[t + "s4"].at[pl.ds(0, 7)])


SHAPES = dict(
    m1=((2, 128, 256), BF),
    z1=((4, 128, 128), F32),
    z2=((4, 128, 128), F32),
    z3=((4, 128, 128), F32),
    msa_out=((2, 128, 256), BF),
)


def out_scratch():
    return tri_scratch("o")


def in_scratch():
    s = tri_scratch("i")
    del s["ips"], s["ipr"]
    s["ipg"] = ((4, 128, 512), BF)
    return s


PARTS = dict(
    row=dict(ins=["msa", "pairs", "row_w", "row_out", "pair_bias"], outs=["m1"], scratch=ROW_SCRATCH, sems=ROW_SEMS),
    col=dict(
        ins=["m1", "pairs", "col_w", "col_out", "maps", "outer_out"],
        outs=["msa_out", "z1"],
        scratch=COL_SCRATCH,
        sems=COL_SEMS,
    ),
    out=dict(ins=["z1", "o_proj", "o_out"], outs=["z2"], scratch=out_scratch(), sems=tri_sems("o")),
    inc=dict(ins=["z2", "i_proj", "i_out"], outs=["z3"], scratch=in_scratch(), sems=tri_sems("i")),
)


def run_parts(parts, arrays, results, number):
    ins, made, scratch, sems = [], [], {}, []
    for p in parts:
        spec = PARTS[p]
        ins += [n for n in spec["ins"] if n not in ins and n not in made]
        made += spec["outs"]
        scratch.update(spec["scratch"])
        sems += spec["sems"]
    outs = [n for n in made if n in results]
    inner = {n: SHAPES[n] for n in made if n not in results}
    scratch = {**scratch, **inner}
    sem_names = [s + e for s in sems for e in ("_s", "_r")]

    def body(*refs):
        r = dict(zip(ins + outs + list(scratch) + sem_names, refs))
        barrier_signal()

        def prep():
            if "col" in parts:
                col_prep(r)
            if "out" in parts:
                tri_prep(r, "o")
            if "inc" in parts:
                tri_prep(r, "i")

        if parts[0] == "row":
            r["prep"] = prep
        else:
            prep()
            barrier_wait()
        for p in parts:
            if p == "row":
                row_part(r)
            elif p == "col":
                col_part(r)
            elif p == "out":
                tri_part(r, "o", "z1", "z2", True)
            else:
                tri_part(r, "i", "z2", "z3", False)

    vm = pl.BlockSpec(memory_space=pltpu.VMEM)
    got = pl.pallas_call(
        body,
        out_shape=[jax.ShapeDtypeStruct(*SHAPES[n]) for n in outs],
        in_specs=[vm] * len(ins),
        out_specs=[vm] * len(outs),
        scratch_shapes=[pltpu.VMEM(*scratch[n]) for n in scratch] + [pltpu.SemaphoreType.DMA] * len(sem_names),
        compiler_params=pltpu.CompilerParams(
            collective_id=number, has_side_effects=True, vmem_limit_bytes=56 * 1024 * 1024
        ),
        name="_".join(parts),
    )(*[arrays[n] for n in ins])
    arrays.update(zip(outs, got))


GROUPS = [["row", "col", "out", "inc"]]


def shards(*args, groups=None, results=("msa_out", "z3")):
    groups = groups or GROUPS
    names = ["msa", "pairs", "row_w", "row_out", "pair_bias", "col_w", "col_out", "maps", "outer_out"]
    names += ["o_proj", "o_out", "i_proj", "i_out"]
    arrays = dict(zip(names, args))
    msa_shape, pair_shape = arrays["msa"].shape, arrays["pairs"].shape
    arrays["msa"] = arrays["msa"].reshape(2, 128, 256)
    arrays["pairs"] = arrays["pairs"].reshape(4, 128, 128)
    for number, group in enumerate(groups):
        later = [n for g in groups[number + 1 :] for p in g for n in PARTS[p]["ins"]]
        run_parts(group, arrays, set(results) | set(later), number)
    outs = dict(
        msa_out=lambda a: a.reshape(msa_shape),
        z3=lambda a: a.reshape(pair_shape),
    )
    return tuple(outs.get(n, lambda a: a)(arrays[n]) for n in results)


def solution(mesh):
    return jax.shard_map(
        shards,
        mesh=mesh,
        in_specs=(P("row", None, "col", None, None),) * 2 + (P(),) * 11,
        out_specs=(P("row", None, "col", None, None),) * 2,
        check_vma=False,
    )
```

time: 702 us -> 225 us (0.32)
  waiting for transfers between devices: 430 us -> 0 us
  Pallas kernels: 0 us -> 220 us
  blocking collectives: 116 us -> 0 us
  starting transfers between devices: 90.3 us -> 0 us
  local copies, waits for them, and re-layouts: 26.1 us -> 4.46 us
  between operations: 14.7 us -> 0.66 us
  matrix products: 12 us -> 0 us
  other arithmetic: 11.8 us -> 0 us
    all_gather x2 -> x0, waiting for transfers between devices: 340 us -> none  [the longest x1 176 us: shards(): lax.all_gather(outer_ab[..., OUTER_CHANNELS:], 'row', axis=1, tiled=True)]
    pallas_call x0 -> x1, Pallas kernels: none -> 220 us  [run_parts(): pl.pallas_call(body, out_shape=[jax.ShapeDtypeStruct(*SHAPES[n]) for n in...]
    all_to_all x10 -> x0, waiting for transfers between devices: 90.5 us -> none  [the longest x1 21.6 us: shards(): lax.all_to_all(projected, 'col', split_axis=4, concat_axis=2, tiled=True)]
    all_to_all x10 -> x0, starting transfers between devices: 90.3 us -> none  [the longest x2 28 us: triangle(): lax.all_to_all(mixture, 'row', split_axis=1, concat_axis=0, tiled=True)]
    all_gather x3 -> x0, blocking collectives: 66.6 us -> none  [the longest x2 52.1 us: triangle(): lax.all_gather(left_chan.reshape(local_channels, 1, residues, local_colum...]
    all_to_all x2 -> x0, blocking collectives: 49.2 us -> none  [the longest x1 27.8 us: shards(): lax.all_to_all(shortened(gated), 'col', split_axis=2, concat_axis=4, tile...]
    dot_general x19 -> x0, matrix products: 9.43 us -> none  [the longest x2 2.24 us: one_sequence(): jnp.einsum('hij,jhd->ihd', weights, value_rows, preferred_element_type=jn...]
  transfers between devices with their start and end apart: 12 -> 0, of which waited for: 10 -> 0; matrix products, arithmetic and copies ran while one was open for 2% -> 0% of each run, Pallas kernels for 0% -> 0%
where the time goes in v1:
time: 225 us
  Pallas kernels  220 us (98%)
  local copies, waits for them, and re-layouts  4.46 us (2%)
    pallas_call x1, Pallas kernels, run_parts(): pl.pallas_call(body, out_shape=[jax.ShapeDtypeStruct(*SHAPES[n]) for n in...  220 us

profile of v1, /device:TPU:1, one launch (start us, length us, event | category | flops | bytes accessed | tf_op | source)
XLA Modules:
  0.0 225.2 jit_solution(9256176793025359432)
XLA Ops:
  0.6 0.0 copy-start.1
  0.6 1.4 copy.15.refs_4_
  2.0 0.0 copy-done.1
  2.0 0.7 copy.16.refs_7_
  2.8 220.1 %row_col_out_inc.1 = (bf16[2,128,256]{2,1,0:T(8,128)(2,1)}, f32[4,128,128]{2,1,0:T(8,128)}) custom-call(bf16[2,128,256]{2,1,0:T(8,128)(2,1)} %bitcast.9, bf16[4,128,128]{2,1,0:T(8,128)(2,1)} %bitcast.10, bf16[256,1024]{1,0:T(8,128)(2,1)} %refs_2_.1, bf16[256,256]{1,0:T(8,128)(2,1)} %refs_3_.1, bf16[128,8]{1,0:T(8,128)(2,1)} %copy.15.refs_4_, ...), custom_call_target="tpu_custom_call" | custom-call | tf_op jit(solution)/shard_map/row_col_out_inc/pallas_call | solution.py:502
  222.9 0.0 copy-start
  222.9 1.6 copy.21
  224.5 0.0 copy-done
  224.5 0.7 copy.22
Async XLA Ops:
  0.6 1.4 copy-start.1
  222.9 1.6 copy-start

commit v2 on v1

--- a/solution.py
+++ b/solution.py
@@ -58,10 +58,20 @@
     return row, col, row // NZC, row % NZC
 
 
+def in_quad():
+    row, col, xy, zc = where_am_i()
+    return 2 * col + zc // 4, zc % 4
+
+
+def place(xy, m, e):
+    return xy * NZC + m % 2 * 4 + e, m // 2
+
+
 class Swap:
     def __init__(self, r, name):
         self.send, self.recv = r[name + "_s"], r[name + "_r"]
         self.row, self.col, self.xy, self.zc = where_am_i()
+        self.m, self.e = in_quad()
 
     def put(self, src, dst, row, col):
         pltpu.make_async_remote_copy(
@@ -85,13 +95,17 @@
             for d in range(1, NZC):
                 g = lax.rem(self.zc + d, NZC)
                 yield g, self.xy * NZC + g, self.col
+        elif kind == "quad":
+            for d in range(1, 4):
+                g = lax.rem(self.e + d, 4)
+                yield g, *place(self.xy, self.m, g)
         else:
             for d in range(1, NCOL):
                 g = lax.rem(self.col + d, NCOL)
                 yield g, self.row, g
 
     def mine(self, kind):
-        return {"xy": self.xy, "zc": self.zc, "col": self.col}[kind]
+        return {"xy": self.xy, "zc": self.zc, "col": self.col, "quad": self.e}[kind]
 
     def exchange(self, kind, src, dst):
         me = self.mine(kind)
@@ -104,6 +118,43 @@
         for g, row, col in self.peers(kind):
             self.put(buf.at[me], buf.at[me], row, col)
 
+    def ring(self, src_of, dst):
+        here = self.m * 4 + self.e
+        for d in range(1, 32):
+            t = lax.rem(here + d, 32)
+            m, e = t // 4, t % 4
+            self.put(src_of(m, e), dst.at[self.zc, self.col], *place(self.xy, m, e))
+        self.keep(src_of(self.m, self.e), dst.at[self.zc, self.col])
+
+    def either(self, src, dst, away, row, col):
+        @pl.when(away)
+        def _():
+            self.put(src, dst, row, col)
+
+        @pl.when(jnp.logical_not(away))
+        def _():
+            self.keep(src, dst)
+
+    def out(self, src, dst):
+        for d in range(1, 8):
+            m = lax.rem(self.m + d, 8)
+            self.put(src.at[m], dst.at[self.zc], *place(self.xy, m, self.col))
+        row, col = place(self.xy, self.m, self.col)
+        self.either(src.at[self.m], dst.at[self.zc], self.e != self.col, row, col)
+
+    def back(self, src, dst):
+        for d in range(1, 8):
+            g = lax.rem(self.zc + d, 8)
+            self.put(src.at[g], dst.at[self.m], self.xy * NZC + g, self.e)
+        self.either(src.at[self.zc], dst.at[self.m], self.e != self.col, self.row, self.e)
+
+    def sent8(self, src):
+        self.sent(src.at[pl.ds(0, 7)])
+
+        @pl.when(self.e != self.col)
+        def _():
+            self.sent(src.at[0])
+
     def got(self, ref):
         pltpu.make_async_copy(ref, ref, self.recv).wait()
 
@@ -113,6 +164,7 @@
 
 def barrier_signal():
     row, col, xy, zc = where_am_i()
+    m, e = in_quad()
     sem = pltpu.get_barrier_semaphore()
 
     def hail(r, c):
@@ -120,14 +172,13 @@
 
     for d in range(1, NXY):
         hail(lax.rem(xy + d, NXY) * NZC + zc, col)
-    for d in range(1, NZC):
-        hail(xy * NZC + lax.rem(zc + d, NZC), col)
-    for d in range(1, NCOL):
-        hail(row, lax.rem(col + d, NCOL))
+    for d in range(1, 32):
+        t = lax.rem(m * 4 + e + d, 32)
+        hail(*place(xy, t // 4, t % 4))
 
 
 def barrier_wait():
-    pl.semaphore_wait(pltpu.get_barrier_semaphore(), NXY + NZC + NCOL - 3)
+    pl.semaphore_wait(pltpu.get_barrier_semaphore(), NXY + 32 - 2)
 
 
 def attend(keys, own, weights, bias):
@@ -160,46 +211,50 @@
 
 
 ROW_SCRATCH = dict(
+    xr=((2, 128, 256), BF),
     xg=((2, 4, 128, 256), BF),
     bsend=((4, 8, 128), F32),
-    brecv=((4, 8, 128), F32),
-    bz=((8, 16, 256), BF),
+    brecv=((8, 4, 8, 128), F32),
     bx=((16, 128, 256), BF),
     wrow=((256, 1024), BF),
 )
-ROW_SEMS = ["m0", "m1", "b0", "b1", "b2"]
+ROW_SEMS = ["m0", "m1", "g0", "g1", "b0", "b2"]
 
 
 def row_part(r):
     row, col, xy, zc = where_am_i()
-    m = r["msa"]
-    x = norm(m[...].astype(F32)).astype(BF)
-    xg = r["xg"]
-    for s in range(2):
-        xg[s, col] = x[s]
-    barrier_wait()
-    swaps = [Swap(r, "m0"), Swap(r, "m1")]
+    m, e = in_quad()
+    msa, xr, xg = r["msa"], r["xr"], r["xg"]
     zn = norm(r["pairs"][...].astype(F32)).astype(BF).reshape(512, 128)
     bias_t = nt(r["pair_bias"][...].T, zn)
     for k in range(4):
         r["bsend"][k] = bias_t[:, 128 * k : 128 * k + 128]
+    barrier_wait()
     s0 = Swap(r, "b0")
-    s0.exchange("col", r["bsend"], r["brecv"])
+    s0.ring(lambda m, e: r["bsend"].at[e], r["brecv"])
+    direct = [Swap(r, "m0"), Swap(r, "m1")]
+    away = jnp.logical_or(zc != m, col != e)
     for s in range(2):
-        swaps[s].gather("col", xg.at[s])
+        direct[s].either(msa.at[s], xr.at[s], away, *place(xy, zc, col))
     r["wrow"][...] = by_kind(r["row_w"])
+    pz = perm((8, 16), (1, 0))
+    shared = [Swap(r, "g0"), Swap(r, "g1")]
+
+    def share(s):
+        direct[s].got(xr.at[s])
+        xg[s, e] = norm(xr[s].astype(F32)).astype(BF)
+        shared[s].gather("quad", xg.at[s])
+
     s0.got(r["brecv"])
     b = r["brecv"]
-    lo = jnp.concatenate([b[0], b[1]], axis=1)
-    hi = jnp.concatenate([b[2], b[3]], axis=1)
-    r["bz"][zc] = jnp.concatenate([lo, hi], axis=0).astype(BF)
-    s1 = Swap(r, "b1")
-    s1.gather("zc", r["bz"])
-    pz = perm((8, 16), (1, 0))
-    s1.got(r["bz"].at[pl.ds(0, 7)])
-    r["bx"][xy] = nn(pz, r["bz"][...].reshape(128, 256)).astype(BF)
+    lo = jnp.concatenate([b[:, 0], b[:, 1]], axis=2)
+    hi = jnp.concatenate([b[:, 2], b[:, 3]], axis=2)
+    rows = jnp.concatenate([lo, hi], axis=1).astype(BF).reshape(128, 256)
+    r["bx"][xy] = nn(pz, rows).astype(BF)
     s2 = Swap(r, "b2")
     s2.gather("xy", r["bx"])
+    share(0)
+    share(1)
     if "prep" in r:
         r["prep"]()
     s2.got(r["bx"].at[pl.ds(0, 15)])
@@ -219,26 +274,31 @@
         return cache[h]
 
     for s in range(2):
-        swaps[s].got(xg.at[s, pl.ds(0, 3)])
+        shared[s].got(xg.at[s, pl.ds(0, 3)])
         cache.clear()
-        gated = attend(xg[s].reshape(512, 256), xg[s, col], r["wrow"], bias)
-        r["m1"][s] = (m[s].astype(F32) + nn(gated, r["row_out"][...])).astype(BF)
+        gated = attend(xg[s].reshape(512, 256), xg[s, e], r["wrow"], bias)
+        r["m1"][s] = (xr[s].astype(F32) + nn(gated, r["row_out"][...])).astype(BF)
     for s in range(2):
-        swaps[s].sent(xg.at[s, pl.ds(0, 3)])
-    s0.sent(r["bsend"].at[pl.ds(0, 3)])
-    s1.sent(r["bz"].at[pl.ds(0, 7)])
+        shared[s].sent(xg.at[s, pl.ds(0, 3)])
+
+        @pl.when(away)
+        def _():
+            direct[s].sent(msa.at[s])
+
+    s0.sent(r["brecv"].at[pl.ds(0, 7)])
+    s0.sent(r["brecv"].at[0, pl.ds(0, 3)])
     s2.sent(r["bx"].at[pl.ds(0, 15)])
 
 
 COL_SCRATCH = dict(
-    cs1=((16, 16, 256), BF),
-    cr1=((16, 16, 256), BF),
-    cs2=((8, 32, 256), BF),
-    cr2=((8, 32, 256), BF),
-    ds1=((8, 32, 256), BF),
-    dr1=((8, 32, 256), BF),
-    ds2=((16, 16, 256), BF),
-    dr2=((16, 16, 256), BF),
+    cs1=((8, 32, 256), BF),
+    cr1=((8, 32, 256), BF),
+    cs2=((16, 16, 256), BF),
+    cr2=((16, 16, 256), BF),
+    ds1=((16, 16, 256), BF),
+    dr1=((16, 16, 256), BF),
+    ds2=((8, 32, 256), BF),
+    dr2=((8, 32, 256), BF),
     lg=((4, 32, 256), BF),
     rz=((8, 32, 256), BF),
     rx=((16, 256, 256), BF),
@@ -259,15 +319,14 @@
 def col_part(r):
     row, col, xy, zc = where_am_i()
     core = lax.rem(zc, 2)
-    m1 = r["m1"][...].astype(F32).reshape(2, 16, 8, 256)
-    r["cs1"][...] = jnp.concatenate([m1[0], m1[1]], axis=1).astype(BF)
+    r["cs1"][...] = nn(perm((2, 16, 8), (2, 0, 1)), r["m1"][...].reshape(256, 256)).astype(BF).reshape(8, 32, 256)
     c1 = Swap(r, "c1")
-    c1.exchange("xy", r["cs1"], r["cr1"])
-    to_zc = perm((16, 2, 8), (2, 0, 1))
+    c1.back(r["cs1"], r["cr1"])
+    to_xy = perm((8, 2, 16), (2, 0, 1))
     c1.got(r["cr1"])
-    r["cs2"][...] = nn(to_zc, r["cr1"][...].reshape(256, 256)).astype(BF).reshape(8, 32, 256)
+    r["cs2"][...] = nn(to_xy, r["cr1"][...].reshape(256, 256)).astype(BF).reshape(16, 16, 256)
     c2 = Swap(r, "c2")
-    c2.exchange("zc", r["cs2"], r["cr2"])
+    c2.exchange("xy", r["cs2"], r["cr2"])
     c2.got(r["cr2"])
     lines = r["cr2"][...].reshape(256, 256).astype(F32)
     x = norm(lines).astype(BF)
@@ -281,9 +340,9 @@
     rz.gather("zc", r["rz"])
     lg = Swap(r, "lg")
     lg.gather("col", r["lg"])
-    r["ds1"][...] = m2.astype(BF).reshape(8, 32, 256)
+    r["ds1"][...] = m2.astype(BF).reshape(16, 16, 256)
     d1 = Swap(r, "d1")
-    d1.exchange("zc", r["ds1"], r["dr1"])
+    d1.exchange("xy", r["ds1"], r["dr1"])
     rz.got(r["rz"].at[pl.ds(0, 7)])
     right = nn(perm((8, 32), (1, 0)), r["rz"][...].reshape(256, 256)).astype(BF)
     rx = r["rx"]
@@ -299,18 +358,18 @@
     for g, prow, pcol in rxs.peers("xy"):
         rxs.put(rx.at[xy, half], rx.at[xy, half], prow, pcol)
     d1.got(r["dr1"])
-    r["ds2"][...] = nn(perm((8, 16, 2), (1, 2, 0)), r["dr1"][...].reshape(256, 256)).astype(BF).reshape(16, 16, 256)
+    r["ds2"][...] = nn(perm((16, 8, 2), (1, 2, 0)), r["dr1"][...].reshape(256, 256)).astype(BF).reshape(8, 32, 256)
     d2 = Swap(r, "d2")
-    d2.exchange("xy", r["ds2"], r["dr2"])
+    d2.exchange("zc", r["ds2"], r["dr2"])
     lg.got(r["lg"].at[pl.ds(0, 3)])
     left = r["lg"][...].reshape(128, 256).T
     rxs.got(rx.at[pl.ds(0, 15), pl.ds(0, 128)])
     rc = Swap(r, "rc")
     rc.put(rx.at[:, half], rx.at[:, half], row + 1 - 2 * core, col)
     d2.got(r["dr2"])
-    dr2 = r["dr2"][...].astype(F32)
-    for s in range(2):
-        r["msa_out"][s] = dr2[:, 8 * s : 8 * s + 8].reshape(128, 256).astype(BF)
+    r["msa_out"][...] = (
+        nn(perm((8, 2, 16), (1, 2, 0)), r["dr2"][...].reshape(256, 256)).astype(BF).reshape(2, 128, 256)
+    )
 
     def add(base, acc):
         for up in range(8):
@@ -326,32 +385,31 @@
     acc = add(16 - core * 16, acc)
     for i in range(4):
         r["z1"][i] = r["pairs"][i].astype(F32) + acc[:, 128 * i : 128 * i + 128] * (1.0 / 256.0)
-    c1.sent(r["cs1"].at[pl.ds(0, 15)])
-    c2.sent(r["cs2"].at[pl.ds(0, 7)])
-    d1.sent(r["ds1"].at[pl.ds(0, 7)])
-    d2.sent(r["ds2"].at[pl.ds(0, 15)])
+    c1.sent8(r["cs1"])
+    c2.sent(r["cs2"].at[pl.ds(0, 15)])
+    d1.sent(r["ds1"].at[pl.ds(0, 15)])
+    d2.sent(r["ds2"].at[pl.ds(0, 7)])
     lg.sent(r["lg"].at[pl.ds(0, 3)])
     rz.sent(r["rz"].at[pl.ds(0, 7)])
     rxs.sent(rx.at[pl.ds(0, 15), pl.ds(0, 128)])
     rc.sent(rx.at[:, half])
 
 
-def tri_scratch(t):
+def tri_scratch(t, outgoing):
     return {
         t + "s1": ((16, 16, 512), BF),
         t + "r1": ((16, 16, 512), BF),
         t + "s2": ((8, 32, 512), BF),
-        t + "r2": ((8, 32, 512), BF),
+        t + "r2": ((8, 32, 512) if outgoing else (8, 4, 32, 128), BF),
         t + "ps": ((4, 512, 128), BF),
         t + "pr": ((4, 512, 128), BF),
-        t + "s3": ((16, 32, 128), BF),
-        t + "r3": ((16, 32, 128), BF),
-        t + "s4": ((8, 64, 128), BF),
-        t + "r4": ((8, 64, 128), BF),
+        t + "s3": ((8, 64, 128), BF),
+        t + "r3": ((8, 64, 128), BF),
+        t + "s4": ((16, 32, 128), BF),
+        t + "r4": ((16, 32, 128), BF),
         t + "gate": ((512, 128), F32),
         t + "wg": ((256, 128), BF),
         t + "wv": ((256, 128), BF),
-        t + "wo": ((128, 128), BF),
     }
 
 
@@ -363,66 +421,71 @@
     w = r[t + "_proj"][:, 0:512].astype(F32).T.reshape(4, 16, 8, 128)
     r[t + "wg"][...] = jnp.concatenate([w[0], w[2]], axis=1).astype(BF).reshape(256, 128)
     r[t + "wv"][...] = jnp.concatenate([w[1], w[3]], axis=1).astype(BF).reshape(256, 128)
-    r[t + "wo"][...] = nn(perm((16, 8), (1, 0)), r[t + "_out"][...]).astype(BF)
 
 
 def tri_part(r, t, src, dst, outgoing):
     row, col, xy, zc = where_am_i()
+    m, e = in_quad()
     x = norm(r[src][...]).astype(BF).reshape(512, 128)
     both = sig(nt(r[t + "wg"][...], x)) * nt(r[t + "wv"][...], x)
-    r[t + "s1"][...] = both.astype(BF).reshape(16, 16, 512)
+    s1, r1, s2, r2 = (r[t + k] for k in ("s1", "r1", "s2", "r2"))
+    s1[...] = both.astype(BF).reshape(16, 16, 512)
     e1 = Swap(r, t + "1")
-    e1.exchange("xy", r[t + "s1"], r[t + "r1"])
+    e1.exchange("xy", s1, r1)
     r[t + "gate"][...] = sig(nn(x, r[t + "_proj"][:, 512:640]))
-    to_zc = perm((16, 2, 8), (2, 1, 0))
-    e1.got(r[t + "r1"])
-    r[t + "s2"][...] = nn(to_zc, r[t + "r1"][...].reshape(256, 512)).astype(BF).reshape(8, 32, 512)
+    by_quad = perm((16, 2, 8), (2, 1, 0))
+    e1.got(r1)
+    s2[...] = nn(by_quad, r1[...].reshape(256, 512)).astype(BF).reshape(8, 32, 512)
     e2 = Swap(r, t + "2")
-    e2.exchange("zc", r[t + "s2"], r[t + "r2"])
-    natural = perm((8, 16), (1, 0))
-    e2.got(r[t + "r2"])
-    left = r[t + "r2"][:, 0:16, :].reshape(128, 512)
-    right = r[t + "r2"][:, 16:32, :].reshape(128, 512)
+    if outgoing:
+        e2.out(s2, r2)
+        natural = perm((8, 16), (1, 0))
+    else:
+        e2.ring(lambda m, e: s2.at[m, :, pl.ds(pl.multiple_of(e * 128, 128), 128)], r2)
+        natural = perm((16, 8), (1, 0))
+    e2.got(r2)
+    ps, pr = r[t + "ps"], r[t + "pr"]
     ep = Swap(r, t + "p")
     if outgoing:
-        left = nn(natural, left).astype(BF)
-        right = nn(natural, right).astype(BF)
+        left = r2[:, 0:16, :].reshape(128, 512)
+        right = nn(natural, r2[:, 16:32, :].reshape(128, 512)).astype(BF)
         left = jnp.concatenate([left[:, 128 * q : 128 * q + 128] for q in range(4)], axis=0)
         for q in range(4):
-            r[t + "ps"][q] = nt(left, right[:, 128 * q : 128 * q + 128]).astype(BF)
-        ep.exchange("col", r[t + "ps"], r[t + "pr"])
-        ep.got(r[t + "pr"])
-        pr = r[t + "pr"]
-        mix = (pr[0].astype(F32) + pr[1].astype(F32)) + (pr[2].astype(F32) + pr[3].astype(F32))
+            ps[q] = nt(left, right[:, 128 * q : 128 * q + 128]).astype(BF)
     else:
-        gathered = r[t + "pg"]
-        gathered[col] = jnp.concatenate([left[:, 128 * q : 128 * q + 128].T for q in range(4)], axis=1)
-        ep.gather("col", gathered)
-        right = jnp.concatenate([right[:, 128 * q : 128 * q + 128] for q in range(4)], axis=0)
-        ep.got(gathered.at[pl.ds(0, 3)])
-        mix = nn(gathered[...].reshape(512, 512), right)
-    mix = mix.reshape(4, 16, 8, 128)
-    r[t + "s3"][...] = jnp.concatenate([mix[q] for q in range(4)], axis=1).astype(BF)
+        left = jnp.concatenate(
+            [nt(natural, r2[:, c, 0:16, :].reshape(128, 128)).astype(BF) for c in range(4)], axis=0
+        )
+        for c in range(4):
+            ps[c] = nn(left, r2[:, c, 16:32, :].reshape(128, 128)).astype(BF)
+    ep.exchange("quad", ps, pr)
+    ep.got(pr)
+    mix = (pr[0].astype(F32) + pr[1].astype(F32)) + (pr[2].astype(F32) + pr[3].astype(F32))
+    mix = mix.astype(BF).reshape(4, 8, 16, 128)
+    s3, r3, s4, r4 = (r[t + k] for k in ("s3", "r3", "s4", "r4"))
+    for q in range(4):
+        s3[:, 16 * q : 16 * q + 16] = mix[q]
     e3 = Swap(r, t + "3")
-    e3.exchange("xy", r[t + "s3"], r[t + "r3"])
-    back = perm((16, 4, 8), (2, 1, 0))
-    e3.got(r[t + "r3"])
-    r[t + "s4"][...] = nn(back, r[t + "r3"][...].reshape(512, 128)).astype(BF).reshape(8, 64, 128)
+    e3.back(s3, r3)
+    by_plane = perm((8, 4, 16), (2, 1, 0))
+    e3.got(r3)
+    s4[...] = nn(by_plane, r3[...].reshape(512, 128)).astype(BF).reshape(16, 32, 128)
     e4 = Swap(r, t + "4")
-    e4.exchange("zc", r[t + "s4"], r[t + "r4"])
-    e4.got(r[t + "r4"])
+    e4.exchange("xy", s4, r4)
+    e4.got(r4)
+    got = r4[...].astype(F32)
     for q in range(4):
-        mq = r[t + "r4"][:, 16 * q : 16 * q + 16, :].reshape(128, 128).astype(F32)
-        step = tn(norm(mq, 0).astype(BF), r[t + "wo"][...])
+        step = tn(norm(got[:, 8 * q : 8 * q + 8].reshape(128, 128), 0).astype(BF), r[t + "_out"][...])
         r[dst][q] = r[src][q] + r[t + "gate"][128 * q : 128 * q + 128] * step
-    e1.sent(r[t + "s1"].at[pl.ds(0, 15)])
-    e2.sent(r[t + "s2"].at[pl.ds(0, 7)])
+    e1.sent(s1.at[pl.ds(0, 15)])
     if outgoing:
-        ep.sent(r[t + "ps"].at[pl.ds(0, 3)])
+        e2.sent8(s2)
     else:
-        ep.sent(r[t + "pg"].at[pl.ds(0, 3)])
-    e3.sent(r[t + "s3"].at[pl.ds(0, 15)])
-    e4.sent(r[t + "s4"].at[pl.ds(0, 7)])
+        e2.sent(r2.at[pl.ds(0, 7)])
+        e2.sent(r2.at[0, pl.ds(0, 3)])
+    ep.sent(ps.at[pl.ds(0, 3)])
+    e3.sent8(s3)
+    e4.sent(s4.at[pl.ds(0, 15)])
 
 
 SHAPES = dict(
@@ -432,17 +495,6 @@
     z3=((4, 128, 128), F32),
     msa_out=((2, 128, 256), BF),
 )
-
-
-def out_scratch():
-    return tri_scratch("o")
-
-
-def in_scratch():
-    s = tri_scratch("i")
-    del s["ips"], s["ipr"]
-    s["ipg"] = ((4, 128, 512), BF)
-    return s
 
 
 PARTS = dict(
@@ -453,8 +505,8 @@
         scratch=COL_SCRATCH,
         sems=COL_SEMS,
     ),
-    out=dict(ins=["z1", "o_proj", "o_out"], outs=["z2"], scratch=out_scratch(), sems=tri_sems("o")),
-    inc=dict(ins=["z2", "i_proj", "i_out"], outs=["z3"], scratch=in_scratch(), sems=tri_sems("i")),
+    out=dict(ins=["z1", "o_proj", "o_out"], outs=["z2"], scratch=tri_scratch("o", True), sems=tri_sems("o")),
+    inc=dict(ins=["z2", "i_proj", "i_out"], outs=["z3"], scratch=tri_scratch("i", False), sems=tri_sems("i")),
 )
 
 

time: 225 us -> 194 us (0.86)
  Pallas kernels: 220 us -> 187 us
    pallas_call x1, Pallas kernels: 220 us -> 187 us  [run_parts(): pl.pallas_call(body, out_shape=[jax.ShapeDtypeStruct(*SHAPES[n]) for n in...]
where the time goes in v2:
time: 194 us; the launch traced here: 192 us
  Pallas kernels  187 us (96%)
  local copies, waits for them, and re-layouts  4.46 us (2%)
    pallas_call x1, Pallas kernels, run_parts(): pl.pallas_call(body, out_shape=[jax.ShapeDtypeStruct(*SHAPES[n]) for n in...  187 us
    unnamed x8, local copies, waits for them, and re-layouts  4.46 us

profile of v2, /device:TPU:1, one launch (start us, length us, event | category | flops | bytes accessed | tf_op | source)
XLA Modules:
  0.0 192.2 jit_solution(11114491822866866350)
XLA Ops:
  0.6 0.0 copy-start.1
  0.6 1.4 copy.15.refs_4_
  2.0 0.0 copy-done.1
  2.0 0.7 copy.16.refs_7_
  2.8 187.1 %row_col_out_inc.1 = (bf16[2,128,256]{2,1,0:T(8,128)(2,1)}, f32[4,128,128]{2,1,0:T(8,128)}) custom-call(bf16[2,128,256]{2,1,0:T(8,128)(2,1)} %bitcast.9, bf16[4,128,128]{2,1,0:T(8,128)(2,1)} %bitcast.10, bf16[256,1024]{1,0:T(8,128)(2,1)} %refs_2_.1, bf16[256,256]{1,0:T(8,128)(2,1)} %refs_3_.1, bf16[128,8]{1,0:T(8,128)(2,1)} %copy.15.refs_4_, ...), custom_call_target="tpu_custom_call" | custom-call | tf_op jit(solution)/shard_map/row_col_out_inc/pallas_call | solution.py:554
  189.9 0.0 copy-start
  189.9 1.6 copy.21
  191.5 0.0 copy-done
  191.5 0.7 copy.22
Async XLA Ops:
  0.6 1.4 copy-start.1
  189.9 1.6 copy-start

commit v3 on v2

--- a/solution.py
+++ b/solution.py
@@ -118,14 +118,6 @@
         for g, row, col in self.peers(kind):
             self.put(buf.at[me], buf.at[me], row, col)
 
-    def ring(self, src_of, dst):
-        here = self.m * 4 + self.e
-        for d in range(1, 32):
-            t = lax.rem(here + d, 32)
-            m, e = t // 4, t % 4
-            self.put(src_of(m, e), dst.at[self.zc, self.col], *place(self.xy, m, e))
-        self.keep(src_of(self.m, self.e), dst.at[self.zc, self.col])
-
     def either(self, src, dst, away, row, col):
         @pl.when(away)
         def _():
@@ -148,6 +140,13 @@
             self.put(src.at[g], dst.at[self.m], self.xy * NZC + g, self.e)
         self.either(src.at[self.zc], dst.at[self.m], self.e != self.col, self.row, self.e)
 
+    def out_by_row(self, src, dst):
+        slot = dst.at[self.zc // 4, self.col]
+        for d in range(1, 8):
+            m = lax.rem(self.m + d, 8)
+            self.put(src.at[m], slot, *place(self.xy, m, self.e))
+        self.keep(src.at[self.m], slot)
+
     def sent8(self, src):
         self.sent(src.at[pl.ds(0, 7)])
 
@@ -181,16 +180,18 @@
     pl.semaphore_wait(pltpu.get_barrier_semaphore(), NXY + 32 - 2)
 
 
-def attend(keys, own, weights, bias):
-    length = keys.shape[0]
+def project(keys, own, weights):
     q = nn(own, weights[:, 0:256]).astype(BF)
     k = nn(keys, weights[:, 256:512]).astype(BF)
     v = nn(keys, weights[:, 512:768]).astype(BF)
     gate = nn(own, weights[:, 768:1024]).astype(BF).astype(F32)
-    v = jnp.concatenate([v, jnp.ones((length, 128), BF)], axis=1)
+    return q, k, jnp.concatenate([v, jnp.ones((keys.shape[0], 128), BF)], axis=1), gate
+
+
+def attend(q, k, v, heads, bias):
     head = lax.broadcasted_iota(jnp.int32, q.shape, 1) // 32
     total = jnp.zeros(q.shape, F32)
-    for h in range(HEADS):
+    for h in heads:
         scores = nt(jnp.where(head == h, q, jnp.zeros_like(q)), k) * (1.0 / math.sqrt(32.0))
         if bias is not None:
             scores = scores + bias(h)
@@ -200,7 +201,7 @@
         inv = 1.0 / mixed[:, 256:384]
         mixed = mixed[:, 0:256] * jnp.concatenate([inv, inv], axis=1)
         total = total + jnp.where(head == h, mixed, 0.0)
-    return (sig(gate) * total).astype(BF)
+    return total
 
 
 def by_kind(ref):
@@ -213,12 +214,14 @@
 ROW_SCRATCH = dict(
     xr=((2, 128, 256), BF),
     xg=((2, 4, 128, 256), BF),
-    bsend=((4, 8, 128), F32),
-    brecv=((8, 4, 8, 128), F32),
+    bs=((2, 2, 8, 128), F32),
+    bo=((2, 8, 128), F32),
+    bq=((2, 16, 128), BF),
+    brecv=((4, 4, 16, 128), BF),
     bx=((16, 128, 256), BF),
     wrow=((256, 1024), BF),
 )
-ROW_SEMS = ["m0", "m1", "g0", "g1", "b0", "b2"]
+ROW_SEMS = ["m0", "m1", "g0", "g1", "bc", "b0", "b2", "b3"]
 
 
 def row_part(r):
@@ -226,18 +229,31 @@
     m, e = in_quad()
     msa, xr, xg = r["msa"], r["xr"], r["xg"]
     zn = norm(r["pairs"][...].astype(F32)).astype(BF).reshape(512, 128)
-    bias_t = nt(r["pair_bias"][...].T, zn)
+    bias_t = nt(r["pair_bias"][...], zn)
     for k in range(4):
-        r["bsend"][k] = bias_t[:, 128 * k : 128 * k + 128]
+        r["bs"][k // 2, k % 2] = bias_t[:, 128 * k : 128 * k + 128]
+    core = lax.rem(zc, 2)
     barrier_wait()
+    sc = Swap(r, "bc")
+    sc.put(r["bs"].at[1 - core], r["bo"], row + 1 - 2 * core, col)
+    sc.got(r["bo"])
+    ours, theirs = r["bs"][core], r["bo"][...]
+    r["bq"][...] = jnp.concatenate(
+        [jnp.where(core == 0, ours, theirs), jnp.where(core == 0, theirs, ours)], axis=1
+    ).astype(BF)
     s0 = Swap(r, "b0")
-    s0.ring(lambda m, e: r["bsend"].at[e], r["brecv"])
+    slot = r["brecv"].at[zc // 2, col]
+    for d in range(1, 8):
+        for k in range(2):
+            s0.put(r["bq"].at[k], slot, *place(xy, lax.rem(m + d, 8), 2 * core + k))
+    for k in range(2):
+        s0.either(r["bq"].at[k], slot, e != 2 * core + k, *place(xy, m, 2 * core + k))
     direct = [Swap(r, "m0"), Swap(r, "m1")]
     away = jnp.logical_or(zc != m, col != e)
     for s in range(2):
         direct[s].either(msa.at[s], xr.at[s], away, *place(xy, zc, col))
     r["wrow"][...] = by_kind(r["row_w"])
-    pz = perm((8, 16), (1, 0))
+    pz = perm((2, 4, 2, 2, 4), (3, 0, 4, 1, 2))
     shared = [Swap(r, "g0"), Swap(r, "g1")]
 
     def share(s):
@@ -247,25 +263,30 @@
 
     s0.got(r["brecv"])
     b = r["brecv"]
-    lo = jnp.concatenate([b[:, 0], b[:, 1]], axis=2)
-    hi = jnp.concatenate([b[:, 2], b[:, 3]], axis=2)
-    rows = jnp.concatenate([lo, hi], axis=1).astype(BF).reshape(128, 256)
+    lo = jnp.concatenate([b[:, 0], b[:, 1]], axis=2).reshape(64, 256)
+    hi = jnp.concatenate([b[:, 2], b[:, 3]], axis=2).reshape(64, 256)
+    rows = jnp.concatenate([lo, hi], axis=0)
     r["bx"][xy] = nn(pz, rows).astype(BF)
-    s2 = Swap(r, "b2")
-    s2.gather("xy", r["bx"])
+    s2 = [Swap(r, "b2"), Swap(r, "b3")]
+    for k in range(2):
+        s2[k].gather("xy", r["bx"].at[:, pl.ds(64 * k, 64)])
     share(0)
     share(1)
     if "prep" in r:
         r["prep"]()
-    s2.got(r["bx"].at[pl.ds(0, 15)])
+    ready = []
+    for s in range(2):
+        shared[s].got(xg.at[s, pl.ds(0, 3)])
+        ready.append(project(xg[s].reshape(512, 256), xg[s, e], r["wrow"]))
     cache = {}
+    to_zc = perm((16, 8), (1, 0))
 
     def bias(h):
         if h not in cache:
             pair = h // 2 * 2
             parts = []
             for jh in range(2):
-                at = (jh * 8 + pair) * 8
+                at = (h // 4 * 8 + jh * 4 + pair % 4) * 8
                 parts.append(r["bx"][:, at : at + 16, :].astype(F32))
             for k in range(2):
                 cache[pair + k] = jnp.concatenate(
@@ -273,21 +294,42 @@
                 )
         return cache[h]
 
-    for s in range(2):
-        shared[s].got(xg.at[s, pl.ds(0, 3)])
-        cache.clear()
-        gated = attend(xg[s].reshape(512, 256), xg[s, e], r["wrow"], bias)
-        r["m1"][s] = (xr[s].astype(F32) + nn(gated, r["row_out"][...])).astype(BF)
-    for s in range(2):
-        shared[s].sent(xg.at[s, pl.ds(0, 3)])
-
-        @pl.when(away)
-        def _():
-            direct[s].sent(msa.at[s])
-
-    s0.sent(r["brecv"].at[pl.ds(0, 7)])
-    s0.sent(r["brecv"].at[0, pl.ds(0, 3)])
-    s2.sent(r["bx"].at[pl.ds(0, 15)])
+    totals = []
+    for part in range(2):
+        s2[part].got(r["bx"].at[pl.ds(0, 15), pl.ds(64 * part, 64)])
+        for s in range(2):
+            q, k, v, gate = ready[s]
+            cache.clear()
+            mixed = attend(q, k, v, range(4 * part, 4 * part + 4), bias)
+            if part == 0:
+                totals.append(mixed)
+                continue
+            gated = (sig(gate) * (totals[s] + mixed)).astype(BF)
+            m1 = (xr[s].astype(F32) + nn(gated, r["row_out"][...])).astype(BF)
+            r["cs1"][:, 16 * s : 16 * s + 16] = nn(to_zc, m1).astype(BF).reshape(8, 16, 256)
+            rows = pl.ds(16 * s, 16)
+            Swap(r, "c1" + "ab"[s]).back(r["cs1"].at[:, rows], r["cr1"].at[:, rows])
+    def row_sent():
+        for s in range(2):
+            shared[s].sent(xg.at[s, pl.ds(0, 3)])
+
+            @pl.when(away)
+            def _():
+                direct[s].sent(msa.at[s])
+
+        s0.sent(r["brecv"].at[pl.ds(0, 3)])
+        s0.sent(r["brecv"].at[0, pl.ds(0, 2)])
+        for k in range(2):
+
+            @pl.when(e != 2 * core + k)
+            def _():
+                s0.sent(r["bq"].at[k])
+
+        sc.sent(r["bo"])
+        for k in range(2):
+            s2[k].sent(r["bx"].at[pl.ds(0, 15), pl.ds(64 * k, 64)])
+
+    return row_sent
 
 
 COL_SCRATCH = dict(
@@ -304,8 +346,9 @@
     rx=((16, 256, 256), BF),
     wcol=((256, 1024), BF),
     bd=((32, 128, 512), BF),
+    at=((32, 256, 512), BF),
 )
-COL_SEMS = ["c1", "c2", "d1", "d2", "lg", "rz", "rx", "rc"]
+COL_SEMS = ["c1a", "c1b", "c2", "d1", "d2", "lg", "rz", "rx", "rc"]
 
 
 def col_prep(r):
@@ -319,21 +362,21 @@
 def col_part(r):
     row, col, xy, zc = where_am_i()
     core = lax.rem(zc, 2)
-    r["cs1"][...] = nn(perm((2, 16, 8), (2, 0, 1)), r["m1"][...].reshape(256, 256)).astype(BF).reshape(8, 32, 256)
-    c1 = Swap(r, "c1")
-    c1.back(r["cs1"], r["cr1"])
     to_xy = perm((8, 2, 16), (2, 0, 1))
-    c1.got(r["cr1"])
+    c1 = [Swap(r, "c1a"), Swap(r, "c1b")]
+    for k in range(2):
+        c1[k].got(r["cr1"].at[:, pl.ds(16 * k, 16)])
     r["cs2"][...] = nn(to_xy, r["cr1"][...].reshape(256, 256)).astype(BF).reshape(16, 16, 256)
     c2 = Swap(r, "c2")
     c2.exchange("xy", r["cs2"], r["cr2"])
     c2.got(r["cr2"])
     lines = r["cr2"][...].reshape(256, 256).astype(F32)
     x = norm(lines).astype(BF)
-    gated = attend(x, x, r["wcol"], None)
+    q, k, v, gate = project(x, x, r["wcol"])
+    gated = (sig(gate) * attend(q, k, v, range(HEADS), None)).astype(BF)
     m2 = lines + nn(gated, r["col_out"][...])
     x = norm(m2).astype(BF)
-    ab = nt(r["maps"][...].T, x).astype(BF)
+    ab = nt(r["maps"][...], x).astype(BF)
     r["lg"][col] = ab[0:32]
     r["rz"][zc] = ab[32:64]
     rz = Swap(r, "rz")
@@ -363,6 +406,8 @@
     d2.exchange("zc", r["ds2"], r["dr2"])
     lg.got(r["lg"].at[pl.ds(0, 3)])
     left = r["lg"][...].reshape(128, 256).T
+    for u in range(32):
+        r["at"][u] = nn(left, r["bd"][u]).astype(BF)
     rxs.got(rx.at[pl.ds(0, 15), pl.ds(0, 128)])
     rc = Swap(r, "rc")
     rc.put(rx.at[:, half], rx.at[:, half], row + 1 - 2 * core, col)
@@ -376,8 +421,7 @@
             at = pl.multiple_of(base * 8 + up * 16, 16)
             block = rx[:, pl.ds(at, 16), :].astype(F32)
             for k in range(2):
-                a = nn(left, r["bd"][base + 2 * up + k]).astype(BF)
-                acc = acc + nn(block[:, 8 * k : 8 * k + 8].reshape(128, 256).astype(BF), a)
+                acc = acc + nn(block[:, 8 * k : 8 * k + 8].reshape(128, 256).astype(BF), r["at"][base + 2 * up + k])
         return acc
 
     acc = add(core * 16, jnp.zeros((128, 512), F32))
@@ -385,14 +429,18 @@
     acc = add(16 - core * 16, acc)
     for i in range(4):
         r["z1"][i] = r["pairs"][i].astype(F32) + acc[:, 128 * i : 128 * i + 128] * (1.0 / 256.0)
-    c1.sent8(r["cs1"])
-    c2.sent(r["cs2"].at[pl.ds(0, 15)])
-    d1.sent(r["ds1"].at[pl.ds(0, 15)])
-    d2.sent(r["ds2"].at[pl.ds(0, 7)])
-    lg.sent(r["lg"].at[pl.ds(0, 3)])
-    rz.sent(r["rz"].at[pl.ds(0, 7)])
-    rxs.sent(rx.at[pl.ds(0, 15), pl.ds(0, 128)])
-    rc.sent(rx.at[:, half])
+    def col_sent():
+        for k in range(2):
+            c1[k].sent8(r["cs1"].at[:, pl.ds(16 * k, 16)])
+        c2.sent(r["cs2"].at[pl.ds(0, 15)])
+        d1.sent(r["ds1"].at[pl.ds(0, 15)])
+        d2.sent(r["ds2"].at[pl.ds(0, 7)])
+        lg.sent(r["lg"].at[pl.ds(0, 3)])
+        rz.sent(r["rz"].at[pl.ds(0, 7)])
+        rxs.sent(rx.at[pl.ds(0, 15), pl.ds(0, 128)])
+        rc.sent(rx.at[:, half])
+
+    return col_sent
 
 
 def tri_scratch(t, outgoing):
@@ -400,7 +448,7 @@
         t + "s1": ((16, 16, 512), BF),
         t + "r1": ((16, 16, 512), BF),
         t + "s2": ((8, 32, 512), BF),
-        t + "r2": ((8, 32, 512) if outgoing else (8, 4, 32, 128), BF),
+        t + "r2": ((8, 32, 512) if outgoing else (2, 4, 32, 512), BF),
         t + "ps": ((4, 512, 128), BF),
         t + "pr": ((4, 512, 128), BF),
         t + "s3": ((8, 64, 128), BF),
@@ -414,7 +462,7 @@
 
 
 def tri_sems(t):
-    return [t + k for k in ("1", "2", "p", "3", "4")]
+    return [t + k for k in ("1", "2", "p0", "p1", "30", "31", "40", "41")]
 
 
 def tri_prep(r, t):
@@ -441,55 +489,72 @@
         e2.out(s2, r2)
         natural = perm((8, 16), (1, 0))
     else:
-        e2.ring(lambda m, e: s2.at[m, :, pl.ds(pl.multiple_of(e * 128, 128), 128)], r2)
+        e2.out_by_row(s2, r2)
         natural = perm((16, 8), (1, 0))
     e2.got(r2)
     ps, pr = r[t + "ps"], r[t + "pr"]
-    ep = Swap(r, t + "p")
+    s3, r3, s4, r4 = (r[t + k] for k in ("s3", "r3", "s4", "r4"))
     if outgoing:
         left = r2[:, 0:16, :].reshape(128, 512)
         right = nn(natural, r2[:, 16:32, :].reshape(128, 512)).astype(BF)
         left = jnp.concatenate([left[:, 128 * q : 128 * q + 128] for q in range(4)], axis=0)
-        for q in range(4):
-            ps[q] = nt(left, right[:, 128 * q : 128 * q + 128]).astype(BF)
+        right = [right[:, 128 * q : 128 * q + 128] for q in range(4)]
     else:
-        left = jnp.concatenate(
-            [nt(natural, r2[:, c, 0:16, :].reshape(128, 128)).astype(BF) for c in range(4)], axis=0
-        )
+
+        def side(c, at):
+            block = r2[:, c, at : at + 16, :].reshape(32, 512)
+            return jnp.concatenate([block[:, 128 * q : 128 * q + 128] for q in range(4)], axis=0)
+
+        left = jnp.concatenate([nt(natural, side(c, 0)).astype(BF) for c in range(4)], axis=0)
+        right = [side(c, 16) for c in range(4)]
+    ep = [Swap(r, t + "p0"), Swap(r, t + "p1")]
+    e3 = [Swap(r, t + "30"), Swap(r, t + "31")]
+    e4 = [Swap(r, t + "40"), Swap(r, t + "41")]
+    for half in range(2):
+        rows = pl.ds(256 * half, 256)
+        part = left[256 * half : 256 * half + 256]
         for c in range(4):
-            ps[c] = nn(left, r2[:, c, 16:32, :].reshape(128, 128)).astype(BF)
-    ep.exchange("quad", ps, pr)
-    ep.got(pr)
-    mix = (pr[0].astype(F32) + pr[1].astype(F32)) + (pr[2].astype(F32) + pr[3].astype(F32))
-    mix = mix.astype(BF).reshape(4, 8, 16, 128)
-    s3, r3, s4, r4 = (r[t + k] for k in ("s3", "r3", "s4", "r4"))
-    for q in range(4):
-        s3[:, 16 * q : 16 * q + 16] = mix[q]
-    e3 = Swap(r, t + "3")
-    e3.back(s3, r3)
-    by_plane = perm((8, 4, 16), (2, 1, 0))
-    e3.got(r3)
-    s4[...] = nn(by_plane, r3[...].reshape(512, 128)).astype(BF).reshape(16, 32, 128)
-    e4 = Swap(r, t + "4")
-    e4.exchange("xy", s4, r4)
-    e4.got(r4)
-    got = r4[...].astype(F32)
-    for q in range(4):
-        step = tn(norm(got[:, 8 * q : 8 * q + 8].reshape(128, 128), 0).astype(BF), r[t + "_out"][...])
-        r[dst][q] = r[src][q] + r[t + "gate"][128 * q : 128 * q + 128] * step
-    e1.sent(s1.at[pl.ds(0, 15)])
-    if outgoing:
-        e2.sent8(s2)
-    else:
-        e2.sent(r2.at[pl.ds(0, 7)])
-        e2.sent(r2.at[0, pl.ds(0, 3)])
-    ep.sent(ps.at[pl.ds(0, 3)])
-    e3.sent8(s3)
-    e4.sent(s4.at[pl.ds(0, 15)])
+            ps[c, rows] = (nt if outgoing else nn)(part, right[c]).astype(BF)
+        ep[half].exchange("quad", ps.at[:, rows], pr.at[:, rows])
+    by_plane = perm((8, 2, 16), (2, 1, 0))
+    for half in range(2):
+        rows = pl.ds(256 * half, 256)
+        ep[half].got(pr.at[:, rows])
+        mix = (pr[0, rows].astype(F32) + pr[1, rows].astype(F32)) + (pr[2, rows].astype(F32) + pr[3, rows].astype(F32))
+        mix = mix.astype(BF).reshape(2, 8, 16, 128)
+        for q in range(2):
+            s3[:, 32 * half + 16 * q : 32 * half + 16 * q + 16] = mix[q]
+        rows = pl.ds(32 * half, 32)
+        e3[half].back(s3.at[:, rows], r3.at[:, rows])
+    for half in range(2):
+        rows = pl.ds(32 * half, 32)
+        e3[half].got(r3.at[:, rows])
+        rows4 = pl.ds(16 * half, 16)
+        s4[:, rows4] = nn(by_plane, r3[:, rows].reshape(256, 128)).astype(BF).reshape(16, 16, 128)
+        e4[half].exchange("xy", s4.at[:, rows4], r4.at[:, rows4])
+    for half in range(2):
+        rows4 = pl.ds(16 * half, 16)
+        e4[half].got(r4.at[:, rows4])
+        got = r4[:, rows4].astype(F32)
+        for k in range(2):
+            q = 2 * half + k
+            step = tn(norm(got[:, 8 * k : 8 * k + 8].reshape(128, 128), 0).astype(BF), r[t + "_out"][...])
+            r[dst][q] = r[src][q] + r[t + "gate"][128 * q : 128 * q + 128] * step
+    def tri_sent():
+        e1.sent(s1.at[pl.ds(0, 15)])
+        if outgoing:
+            e2.sent8(s2)
+        else:
+            e2.sent(s2.at[pl.ds(0, 7)])
+        for half in range(2):
+            ep[half].sent(ps.at[pl.ds(0, 3), pl.ds(0, 256)])
+            e3[half].sent8(s3.at[:, pl.ds(32 * half, 32)])
+            e4[half].sent(s4.at[pl.ds(0, 15), pl.ds(0, 16)])
+
+    return tri_sent
 
 
 SHAPES = dict(
-    m1=((2, 128, 256), BF),
     z1=((4, 128, 128), F32),
     z2=((4, 128, 128), F32),
     z3=((4, 128, 128), F32),
@@ -498,9 +563,9 @@
 
 
 PARTS = dict(
-    row=dict(ins=["msa", "pairs", "row_w", "row_out", "pair_bias"], outs=["m1"], scratch=ROW_SCRATCH, sems=ROW_SEMS),
+    row=dict(ins=["msa", "pairs", "row_w", "row_out", "pair_bias"], outs=[], scratch=ROW_SCRATCH, sems=ROW_SEMS),
     col=dict(
-        ins=["m1", "pairs", "col_w", "col_out", "maps", "outer_out"],
+        ins=["pairs", "col_w", "col_out", "maps", "outer_out"],
         outs=["msa_out", "z1"],
         scratch=COL_SCRATCH,
         sems=COL_SEMS,
@@ -540,15 +605,18 @@
         else:
             prep()
             barrier_wait()
+        waits = []
         for p in parts:
             if p == "row":
-                row_part(r)
+                waits.append(row_part(r))
             elif p == "col":
-                col_part(r)
+                waits.append(col_part(r))
             elif p == "out":
-                tri_part(r, "o", "z1", "z2", True)
+                waits.append(tri_part(r, "o", "z1", "z2", True))
             else:
-                tri_part(r, "i", "z2", "z3", False)
+                waits.append(tri_part(r, "i", "z2", "z3", False))
+        for wait in waits:
+            wait()
 
     vm = pl.BlockSpec(memory_space=pltpu.VMEM)
     got = pl.pallas_call(
@@ -574,6 +642,7 @@
     names += ["o_proj", "o_out", "i_proj", "i_out"]
     arrays = dict(zip(names, args))
     msa_shape, pair_shape = arrays["msa"].shape, arrays["pairs"].shape
+    arrays["pair_bias"], arrays["maps"] = arrays["pair_bias"].T, arrays["maps"].T
     arrays["msa"] = arrays["msa"].reshape(2, 128, 256)
     arrays["pairs"] = arrays["pairs"].reshape(4, 128, 128)
     for number, group in enumerate(groups):

time: 194 us -> 184 us (0.948)
  Pallas kernels: 187 us -> 181 us
  local copies, waits for them, and re-layouts: 4.46 us -> 2.32 us
    pallas_call x1, Pallas kernels: 187 us -> 181 us  [run_parts(): pl.pallas_call(body, out_shape=[jax.ShapeDtypeStruct(*SHAPES[n]) for n in...]
    unnamed x8 -> x4, local copies, waits for them, and re-layouts: 4.46 us -> 2.32 us
where the time goes in v3:
time: 184 us
  Pallas kernels  181 us (98%)
  local copies, waits for them, and re-layouts  2.32 us (1%)
    pallas_call x1, Pallas kernels, run_parts(): pl.pallas_call(body, out_shape=[jax.ShapeDtypeStruct(*SHAPES[n]) for n in...  181 us

profile of v3, /device:TPU:1, one launch (start us, length us, event | category | flops | bytes accessed | tf_op | source)
XLA Modules:
  0.0 183.8 jit_solution(2728391631177366563)
XLA Ops:
  0.6 180.9 %row_col_out_inc.1 = (bf16[2,128,256]{2,1,0:T(8,128)(2,1)}, f32[4,128,128]{2,1,0:T(8,128)}) custom-call(bf16[2,128,256]{2,1,0:T(8,128)(2,1)} %bitcast.11, bf16[4,128,128]{2,1,0:T(8,128)(2,1)} %bitcast.12, bf16[256,1024]{1,0:T(8,128)(2,1)} %refs_2_.1, bf16[256,256]{1,0:T(8,128)(2,1)} %refs_3_.1, bf16[8,128]{1,0:T(8,128)(2,1)} %bitcast.15, ...), custom_call_target="tpu_custom_call" | custom-call | tf_op jit(solution)/shard_map/row_col_out_inc/pallas_call | solution.py:622
  181.5 0.0 copy-start
  181.5 1.6 copy.19
  183.1 0.0 copy-done
  183.1 0.7 copy.20
Async XLA Ops:
  181.5 1.6 copy-start

commit v4 on v3

--- a/solution.py
+++ b/solution.py
@@ -40,16 +40,17 @@
     return 1.0 / (1.0 + jnp.exp(-x))
 
 
-def perm(sizes, order):
+def perm(sizes, order, first=0, count=None):
     n = math.prod(sizes)
+    count = count or n
     strides = [math.prod(sizes[k + 1 :]) for k in range(len(sizes))]
-    out = lax.broadcasted_iota(jnp.int32, (n, n), 0)
-    src = jnp.zeros((n, n), jnp.int32)
+    out = lax.broadcasted_iota(jnp.int32, (count, 1), 0) + first
+    src = jnp.zeros((count, 1), jnp.int32)
     rest = out
     for axis in reversed(order):
         src = src + (rest & (sizes[axis] - 1)) * strides[axis]
         rest = lax.shift_right_logical(rest, int(math.log2(sizes[axis])))
-    inp = lax.broadcasted_iota(jnp.int32, (n, n), 1)
+    inp = lax.broadcasted_iota(jnp.int32, (count, n), 1)
     return jnp.where(src == inp, 1.0, 0.0).astype(BF)
 
 
@@ -127,25 +128,30 @@
         def _():
             self.keep(src, dst)
 
-    def out(self, src, dst):
-        for d in range(1, 8):
-            m = lax.rem(self.m + d, 8)
-            self.put(src.at[m], dst.at[self.zc], *place(self.xy, m, self.col))
-        row, col = place(self.xy, self.m, self.col)
-        self.either(src.at[self.m], dst.at[self.zc], self.e != self.col, row, col)
+    def direct(self, src, slot, member):
+        core = lax.rem(self.zc, 2)
+        here = self.xy * 4 + self.m // 2
+        for d in range(1, 64):
+            g = lax.rem(here + d, 64)
+            self.put(src.at[g], slot, *place(g // 4, g % 4 * 2 + core, member))
+        row, col = place(self.xy, self.m // 2 * 2 + core, member)
+        self.either(src.at[here], slot, self.elsewhere(member), row, col)
+
+    def elsewhere(self, member):
+        return jnp.logical_or(lax.rem(self.m, 2) != lax.rem(self.zc, 2), self.e != member)
+
+    def sent64(self, src, member):
+        self.sent(src.at[pl.ds(0, 63)])
+
+        @pl.when(self.elsewhere(member))
+        def _():
+            self.sent(src.at[0])
 
     def back(self, src, dst):
         for d in range(1, 8):
             g = lax.rem(self.zc + d, 8)
             self.put(src.at[g], dst.at[self.m], self.xy * NZC + g, self.e)
         self.either(src.at[self.zc], dst.at[self.m], self.e != self.col, self.row, self.e)
-
-    def out_by_row(self, src, dst):
-        slot = dst.at[self.zc // 4, self.col]
-        for d in range(1, 8):
-            m = lax.rem(self.m + d, 8)
-            self.put(src.at[m], slot, *place(self.xy, m, self.e))
-        self.keep(src.at[self.m], slot)
 
     def sent8(self, src):
         self.sent(src.at[pl.ds(0, 7)])
@@ -381,13 +387,12 @@
     r["rz"][zc] = ab[32:64]
     rz = Swap(r, "rz")
     rz.gather("zc", r["rz"])
+    r["ds1"][...] = m2.astype(BF).reshape(16, 16, 256)
+    to_u = perm((8, 32), (1, 0))
     lg = Swap(r, "lg")
+    rz.got(r["rz"].at[pl.ds(0, 7)])
     lg.gather("col", r["lg"])
-    r["ds1"][...] = m2.astype(BF).reshape(16, 16, 256)
-    d1 = Swap(r, "d1")
-    d1.exchange("xy", r["ds1"], r["dr1"])
-    rz.got(r["rz"].at[pl.ds(0, 7)])
-    right = nn(perm((8, 32), (1, 0)), r["rz"][...].reshape(256, 256)).astype(BF)
+    right = nn(to_u, r["rz"][...].reshape(256, 256)).astype(BF)
     rx = r["rx"]
     for k in range(2):
 
@@ -400,10 +405,6 @@
     rxs = Swap(r, "rx")
     for g, prow, pcol in rxs.peers("xy"):
         rxs.put(rx.at[xy, half], rx.at[xy, half], prow, pcol)
-    d1.got(r["dr1"])
-    r["ds2"][...] = nn(perm((16, 8, 2), (1, 2, 0)), r["dr1"][...].reshape(256, 256)).astype(BF).reshape(8, 32, 256)
-    d2 = Swap(r, "d2")
-    d2.exchange("zc", r["ds2"], r["dr2"])
     lg.got(r["lg"].at[pl.ds(0, 3)])
     left = r["lg"][...].reshape(128, 256).T
     for u in range(32):
@@ -411,11 +412,6 @@
     rxs.got(rx.at[pl.ds(0, 15), pl.ds(0, 128)])
     rc = Swap(r, "rc")
     rc.put(rx.at[:, half], rx.at[:, half], row + 1 - 2 * core, col)
-    d2.got(r["dr2"])
-    r["msa_out"][...] = (
-        nn(perm((8, 2, 16), (1, 2, 0)), r["dr2"][...].reshape(256, 256)).astype(BF).reshape(2, 128, 256)
-    )
-
     def add(base, acc):
         for up in range(8):
             at = pl.multiple_of(base * 8 + up * 16, 16)
@@ -429,6 +425,24 @@
     acc = add(16 - core * 16, acc)
     for i in range(4):
         r["z1"][i] = r["pairs"][i].astype(F32) + acc[:, 128 * i : 128 * i + 128] * (1.0 / 256.0)
+    d1, d2 = Swap(r, "d1"), Swap(r, "d2")
+
+    def plane():
+        d1.exchange("xy", r["ds1"], r["dr1"])
+
+    def line():
+        d1.got(r["dr1"])
+        rows = nn(perm((16, 8, 2), (1, 2, 0)), r["dr1"][...].reshape(256, 256))
+        r["ds2"][...] = rows.astype(BF).reshape(8, 32, 256)
+        d2.exchange("zc", r["ds2"], r["dr2"])
+
+    def finish():
+        d2.got(r["dr2"])
+        rows = nn(perm((8, 2, 16), (1, 2, 0)), r["dr2"][...].reshape(256, 256))
+        r["msa_out"][...] = rows.astype(BF).reshape(2, 128, 256)
+
+    r["later"] = [plane, line, finish]
+
     def col_sent():
         for k in range(2):
             c1[k].sent8(r["cs1"].at[:, pl.ds(16 * k, 16)])
@@ -445,10 +459,10 @@
 
 def tri_scratch(t, outgoing):
     return {
-        t + "s1": ((16, 16, 512), BF),
-        t + "r1": ((16, 16, 512), BF),
-        t + "s2": ((8, 32, 512), BF),
-        t + "r2": ((8, 32, 512) if outgoing else (2, 4, 32, 512), BF),
+        t + "f": ((1024, 128), F32),
+        t + "h": ((512, 128), F32),
+        t + "s2": ((64, 16, 128), BF),
+        t + "r2": ((16, 4, 16, 128), BF),
         t + "ps": ((4, 512, 128), BF),
         t + "pr": ((4, 512, 128), BF),
         t + "s3": ((8, 64, 128), BF),
@@ -466,9 +480,12 @@
 
 
 def tri_prep(r, t):
-    w = r[t + "_proj"][:, 0:512].astype(F32).T.reshape(4, 16, 8, 128)
-    r[t + "wg"][...] = jnp.concatenate([w[0], w[2]], axis=1).astype(BF).reshape(256, 128)
-    r[t + "wv"][...] = jnp.concatenate([w[1], w[3]], axis=1).astype(BF).reshape(256, 128)
+    by_core = perm((16, 4, 2), (2, 0, 1))
+    w = r[t + "_proj"]
+    for k in range(2):
+        rows = pl.ds(128 * k, 128)
+        r[t + "wg"][rows] = nt(by_core, w[:, 256 * k : 256 * k + 128]).astype(BF)
+        r[t + "wv"][rows] = nt(by_core, w[:, 256 * k + 128 : 256 * k + 256]).astype(BF)
 
 
 def tri_part(r, t, src, dst, outgoing):
@@ -476,37 +493,44 @@
     m, e = in_quad()
     x = norm(r[src][...]).astype(BF).reshape(512, 128)
     both = sig(nt(r[t + "wg"][...], x)) * nt(r[t + "wv"][...], x)
-    s1, r1, s2, r2 = (r[t + k] for k in ("s1", "r1", "s2", "r2"))
-    s1[...] = both.astype(BF).reshape(16, 16, 512)
+    core = lax.rem(zc, 2)
+    f, h, s2, r2 = (r[t + k] for k in ("f", "h", "s2", "r2"))
+    for k in range(2):
+        for q in range(4):
+            f[pl.ds(4 * k + q, 128, stride=8), :] = both[128 * k : 128 * k + 128, 128 * q : 128 * q + 128]
     e1 = Swap(r, t + "1")
-    e1.exchange("xy", s1, r1)
+    theirs = f.at[pl.ds(pl.multiple_of(512 - core * 512, 512), 512)]
+    e1.put(theirs, h, row + 1 - 2 * core, col)
     r[t + "gate"][...] = sig(nn(x, r[t + "_proj"][:, 512:640]))
-    by_quad = perm((16, 2, 8), (2, 1, 0))
-    e1.got(r1)
-    s2[...] = nn(by_quad, r1[...].reshape(256, 512)).astype(BF).reshape(8, 32, 512)
+    ours = f[pl.ds(pl.multiple_of(core * 512, 512), 512), :].reshape(64, 8, 128)
+    e1.got(h)
+    other = h[...].reshape(64, 8, 128)
+    s2[...] = jnp.concatenate(
+        [jnp.where(core == 0, ours, other), jnp.where(core == 0, other, ours)], axis=1
+    ).astype(BF)
     e2 = Swap(r, t + "2")
+    member, slot = (col, zc // 2) if outgoing else (zc // 2, col)
+    e2.direct(s2, r2.at[xy, slot], member)
     if outgoing:
-        e2.out(s2, r2)
-        natural = perm((8, 16), (1, 0))
+        r["later"][0]()
+        to_left = perm((16, 4, 2, 2, 4), (3, 4, 1, 2, 0), 0, 512)
+        to_right = perm((16, 4, 2, 2, 4), (3, 4, 0, 1, 2), 512, 512)
     else:
-        e2.out_by_row(s2, r2)
+        r["later"][2]()
+        to_both = perm((16, 4, 2, 2, 4), (3, 1, 0, 2, 4))
         natural = perm((16, 8), (1, 0))
     e2.got(r2)
+    landed = r2[...].reshape(1024, 128)
     ps, pr = r[t + "ps"], r[t + "pr"]
     s3, r3, s4, r4 = (r[t + k] for k in ("s3", "r3", "s4", "r4"))
     if outgoing:
-        left = r2[:, 0:16, :].reshape(128, 512)
-        right = nn(natural, r2[:, 16:32, :].reshape(128, 512)).astype(BF)
-        left = jnp.concatenate([left[:, 128 * q : 128 * q + 128] for q in range(4)], axis=0)
-        right = [right[:, 128 * q : 128 * q + 128] for q in range(4)]
+        left = nn(to_left, landed).astype(BF)
+        right = nn(to_right, landed).astype(BF)
     else:
-
-        def side(c, at):
-            block = r2[:, c, at : at + 16, :].reshape(32, 512)
-            return jnp.concatenate([block[:, 128 * q : 128 * q + 128] for q in range(4)], axis=0)
-
-        left = jnp.concatenate([nt(natural, side(c, 0)).astype(BF) for c in range(4)], axis=0)
-        right = [side(c, 16) for c in range(4)]
+        rows = nn(to_both, landed).astype(BF)
+        left = jnp.concatenate([nt(natural, rows[128 * c : 128 * c + 128]).astype(BF) for c in range(4)], axis=0)
+        right = rows[512:1024]
+    right = [right[128 * c : 128 * c + 128] for c in range(4)]
     ep = [Swap(r, t + "p0"), Swap(r, t + "p1")]
     e3 = [Swap(r, t + "30"), Swap(r, t + "31")]
     e4 = [Swap(r, t + "40"), Swap(r, t + "41")]
@@ -532,6 +556,8 @@
         rows4 = pl.ds(16 * half, 16)
         s4[:, rows4] = nn(by_plane, r3[:, rows].reshape(256, 128)).astype(BF).reshape(16, 16, 128)
         e4[half].exchange("xy", s4.at[:, rows4], r4.at[:, rows4])
+    if outgoing:
+        r["later"][1]()
     for half in range(2):
         rows4 = pl.ds(16 * half, 16)
         e4[half].got(r4.at[:, rows4])
@@ -541,11 +567,8 @@
             step = tn(norm(got[:, 8 * k : 8 * k + 8].reshape(128, 128), 0).astype(BF), r[t + "_out"][...])
             r[dst][q] = r[src][q] + r[t + "gate"][128 * q : 128 * q + 128] * step
     def tri_sent():
-        e1.sent(s1.at[pl.ds(0, 15)])
-        if outgoing:
-            e2.sent8(s2)
-        else:
-            e2.sent(s2.at[pl.ds(0, 7)])
+        e1.sent(h)
+        e2.sent64(s2, member)
         for half in range(2):
             ep[half].sent(ps.at[pl.ds(0, 3), pl.ds(0, 256)])
             e3[half].sent8(s3.at[:, pl.ds(32 * half, 32)])

time: 184 us -> 179 us (0.973)
  Pallas kernels: 181 us -> 176 us
    pallas_call x1, Pallas kernels: 181 us -> 176 us  [run_parts(): pl.pallas_call(body, out_shape=[jax.ShapeDtypeStruct(*SHAPES[n]) for n in...]
where the time goes in v4:
time: 179 us
  Pallas kernels  176 us (98%)
  local copies, waits for them, and re-layouts  2.32 us (1%)
    pallas_call x1, Pallas kernels, run_parts(): pl.pallas_call(body, out_shape=[jax.ShapeDtypeStruct(*SHAPES[n]) for n in...  176 us

profile of v4, /device:TPU:1, one launch (start us, length us, event | category | flops | bytes accessed | tf_op | source)
XLA Modules:
  0.0 179.2 jit_solution(16613176341316676723)
XLA Ops:
  0.6 176.2 %row_col_out_inc.1 = (bf16[2,128,256]{2,1,0:T(8,128)(2,1)}, f32[4,128,128]{2,1,0:T(8,128)}) custom-call(bf16[2,128,256]{2,1,0:T(8,128)(2,1)} %bitcast.11, bf16[4,128,128]{2,1,0:T(8,128)(2,1)} %bitcast.12, bf16[256,1024]{1,0:T(8,128)(2,1)} %refs_2_.1, bf16[256,256]{1,0:T(8,128)(2,1)} %refs_3_.1, bf16[8,128]{1,0:T(8,128)(2,1)} %bitcast.15, ...), custom_call_target="tpu_custom_call" | custom-call | tf_op jit(solution)/shard_map/row_col_out_inc/pallas_call | solution.py:645
  176.9 0.0 copy-start
  176.9 1.6 copy.19
  178.5 0.0 copy-done
  178.5 0.7 copy.20
Async XLA Ops:
  176.9 1.6 copy-start

commit v5 on v4

--- a/solution.py
+++ b/solution.py
@@ -227,7 +227,7 @@
     bx=((16, 128, 256), BF),
     wrow=((256, 1024), BF),
 )
-ROW_SEMS = ["m0", "m1", "g0", "g1", "bc", "b0", "b2", "b3"]
+ROW_SEMS = ["m0", "m1", "g0", "g1", "bc", "b0", "h0", "h1", "h2", "h3"]
 
 
 def row_part(r):
@@ -259,7 +259,7 @@
     for s in range(2):
         direct[s].either(msa.at[s], xr.at[s], away, *place(xy, zc, col))
     r["wrow"][...] = by_kind(r["row_w"])
-    pz = perm((2, 4, 2, 2, 4), (3, 0, 4, 1, 2))
+    pz = perm((2, 4, 2, 4, 2), (3, 0, 4, 1, 2))
     shared = [Swap(r, "g0"), Swap(r, "g1")]
 
     def share(s):
@@ -273,9 +273,9 @@
     hi = jnp.concatenate([b[:, 2], b[:, 3]], axis=2).reshape(64, 256)
     rows = jnp.concatenate([lo, hi], axis=0)
     r["bx"][xy] = nn(pz, rows).astype(BF)
-    s2 = [Swap(r, "b2"), Swap(r, "b3")]
-    for k in range(2):
-        s2[k].gather("xy", r["bx"].at[:, pl.ds(64 * k, 64)])
+    s2 = [Swap(r, "h%d" % k) for k in range(4)]
+    for k in range(4):
+        s2[k].gather("xy", r["bx"].at[:, pl.ds(32 * k, 32)])
     share(0)
     share(1)
     if "prep" in r:
@@ -292,7 +292,7 @@
             pair = h // 2 * 2
             parts = []
             for jh in range(2):
-                at = (h // 4 * 8 + jh * 4 + pair % 4) * 8
+                at = (h // 2 * 4 + jh * 2) * 8
                 parts.append(r["bx"][:, at : at + 16, :].astype(F32))
             for k in range(2):
                 cache[pair + k] = jnp.concatenate(
@@ -300,17 +300,17 @@
                 )
         return cache[h]
 
-    totals = []
-    for part in range(2):
-        s2[part].got(r["bx"].at[pl.ds(0, 15), pl.ds(64 * part, 64)])
+    totals = [0.0, 0.0]
+    for part in range(4):
+        s2[part].got(r["bx"].at[pl.ds(0, 15), pl.ds(32 * part, 32)])
         for s in range(2):
             q, k, v, gate = ready[s]
             cache.clear()
-            mixed = attend(q, k, v, range(4 * part, 4 * part + 4), bias)
-            if part == 0:
-                totals.append(mixed)
+            mixed = attend(q, k, v, range(2 * part, 2 * part + 2), bias)
+            totals[s] = totals[s] + mixed
+            if part < 3:
                 continue
-            gated = (sig(gate) * (totals[s] + mixed)).astype(BF)
+            gated = (sig(gate) * totals[s]).astype(BF)
             m1 = (xr[s].astype(F32) + nn(gated, r["row_out"][...])).astype(BF)
             r["cs1"][:, 16 * s : 16 * s + 16] = nn(to_zc, m1).astype(BF).reshape(8, 16, 256)
             rows = pl.ds(16 * s, 16)
@@ -332,8 +332,8 @@
                 s0.sent(r["bq"].at[k])
 
         sc.sent(r["bo"])
-        for k in range(2):
-            s2[k].sent(r["bx"].at[pl.ds(0, 15), pl.ds(64 * k, 64)])
+        for k in range(4):
+            s2[k].sent(r["bx"].at[pl.ds(0, 15), pl.ds(32 * k, 32)])
 
     return row_sent
 
@@ -476,7 +476,7 @@
 
 
 def tri_sems(t):
-    return [t + k for k in ("1", "2", "p0", "p1", "30", "31", "40", "41")]
+    return [t + k for k in ("1", "2", "p0", "p1", "p2", "p3", "30", "31", "32", "33", "40", "41")]
 
 
 def tri_prep(r, t):
@@ -531,28 +531,26 @@
         left = jnp.concatenate([nt(natural, rows[128 * c : 128 * c + 128]).astype(BF) for c in range(4)], axis=0)
         right = rows[512:1024]
     right = [right[128 * c : 128 * c + 128] for c in range(4)]
-    ep = [Swap(r, t + "p0"), Swap(r, t + "p1")]
-    e3 = [Swap(r, t + "30"), Swap(r, t + "31")]
+    ep = [Swap(r, t + "p%d" % q) for q in range(4)]
+    e3 = [Swap(r, t + "3%d" % q) for q in range(4)]
     e4 = [Swap(r, t + "40"), Swap(r, t + "41")]
-    for half in range(2):
-        rows = pl.ds(256 * half, 256)
-        part = left[256 * half : 256 * half + 256]
+    for q in range(4):
+        rows = pl.ds(128 * q, 128)
         for c in range(4):
-            ps[c, rows] = (nt if outgoing else nn)(part, right[c]).astype(BF)
-        ep[half].exchange("quad", ps.at[:, rows], pr.at[:, rows])
+            ps[c, rows] = (nt if outgoing else nn)(left[128 * q : 128 * q + 128], right[c]).astype(BF)
+        ep[q].exchange("quad", ps.at[:, rows], pr.at[:, rows])
     by_plane = perm((8, 2, 16), (2, 1, 0))
-    for half in range(2):
-        rows = pl.ds(256 * half, 256)
-        ep[half].got(pr.at[:, rows])
+    for q in range(4):
+        rows = pl.ds(128 * q, 128)
+        ep[q].got(pr.at[:, rows])
         mix = (pr[0, rows].astype(F32) + pr[1, rows].astype(F32)) + (pr[2, rows].astype(F32) + pr[3, rows].astype(F32))
-        mix = mix.astype(BF).reshape(2, 8, 16, 128)
-        for q in range(2):
-            s3[:, 32 * half + 16 * q : 32 * half + 16 * q + 16] = mix[q]
-        rows = pl.ds(32 * half, 32)
-        e3[half].back(s3.at[:, rows], r3.at[:, rows])
+        s3[:, 16 * q : 16 * q + 16] = mix.astype(BF).reshape(8, 16, 128)
+        rows = pl.ds(16 * q, 16)
+        e3[q].back(s3.at[:, rows], r3.at[:, rows])
     for half in range(2):
         rows = pl.ds(32 * half, 32)
-        e3[half].got(r3.at[:, rows])
+        for q in range(2 * half, 2 * half + 2):
+            e3[q].got(r3.at[:, pl.ds(16 * q, 16)])
         rows4 = pl.ds(16 * half, 16)
         s4[:, rows4] = nn(by_plane, r3[:, rows].reshape(256, 128)).astype(BF).reshape(16, 16, 128)
         e4[half].exchange("xy", s4.at[:, rows4], r4.at[:, rows4])
@@ -570,8 +568,9 @@
         e1.sent(h)
         e2.sent64(s2, member)
         for half in range(2):
-            ep[half].sent(ps.at[pl.ds(0, 3), pl.ds(0, 256)])
-            e3[half].sent8(s3.at[:, pl.ds(32 * half, 32)])
+            for q in range(2 * half, 2 * half + 2):
+                ep[q].sent(ps.at[pl.ds(0, 3), pl.ds(0, 128)])
+                e3[q].sent8(s3.at[:, pl.ds(16 * q, 16)])
             e4[half].sent(s4.at[pl.ds(0, 15), pl.ds(0, 16)])
 
     return tri_sent

time: 179 us -> 181 us (1.011)
  Pallas kernels: 176 us -> 178 us
where the time goes in v5:
time: 181 us
  Pallas kernels  178 us (98%)
  local copies, waits for them, and re-layouts  2.32 us (1%)
    pallas_call x1, Pallas kernels, run_parts(): pl.pallas_call(body, out_shape=[jax.ShapeDtypeStruct(*SHAPES[n]) for n in...  178 us

profile of v5, /device:TPU:1, one launch (start us, length us, event | category | flops | bytes accessed | tf_op | source)
XLA Modules:
  0.0 180.6 jit_solution(17852458476150587804)
XLA Ops:
  0.6 177.7 %row_col_out_inc.1 = (bf16[2,128,256]{2,1,0:T(8,128)(2,1)}, f32[4,128,128]{2,1,0:T(8,128)}) custom-call(bf16[2,128,256]{2,1,0:T(8,128)(2,1)} %bitcast.11, bf16[4,128,128]{2,1,0:T(8,128)(2,1)} %bitcast.12, bf16[256,1024]{1,0:T(8,128)(2,1)} %refs_2_.1, bf16[256,256]{1,0:T(8,128)(2,1)} %refs_3_.1, bf16[8,128]{1,0:T(8,128)(2,1)} %bitcast.15, ...), custom_call_target="tpu_custom_call" | custom-call | tf_op jit(solution)/shard_map/row_col_out_inc/pallas_call | solution.py:644
  178.3 0.0 copy-start
  178.3 1.6 copy.19
  179.9 0.0 copy-done
  179.9 0.7 copy.20
Async XLA Ops:
  178.3 1.6 copy-start

commit v6 on v4

--- a/solution.py
+++ b/solution.py
@@ -224,10 +224,10 @@
     bo=((2, 8, 128), F32),
     bq=((2, 16, 128), BF),
     brecv=((4, 4, 16, 128), BF),
-    bx=((16, 128, 256), BF),
+    bx=((4, 4, 128, 256), BF),
     wrow=((256, 1024), BF),
 )
-ROW_SEMS = ["m0", "m1", "g0", "g1", "bc", "b0", "b2", "b3"]
+ROW_SEMS = ["m0", "m1", "g0", "g1", "bc", "b0", "b1", "b2", "b3"]
 
 
 def row_part(r):
@@ -272,12 +272,31 @@
     lo = jnp.concatenate([b[:, 0], b[:, 1]], axis=2).reshape(64, 256)
     hi = jnp.concatenate([b[:, 2], b[:, 3]], axis=2).reshape(64, 256)
     rows = jnp.concatenate([lo, hi], axis=0)
-    r["bx"][xy] = nn(pz, rows).astype(BF)
+    bx, y, x = r["bx"], xy // 4, xy % 4
+    bx[y, x] = nn(pz, rows).astype(BF)
     s2 = [Swap(r, "b2"), Swap(r, "b3")]
-    for k in range(2):
-        s2[k].gather("xy", r["bx"].at[:, pl.ds(64 * k, 64)])
+    near = Swap(r, "b1")
+    for d in range(1, 4):
+        to = lax.rem(y + d * core, 4) * 4 + lax.rem(x + d - d * core, 4)
+        near.put(bx.at[y, x], bx.at[y, x], to * NZC + zc, col)
     share(0)
     share(1)
+    near.got(bx.at[0, pl.ds(0, 3)])
+
+    @pl.when(core == 0)
+    def _():
+        for k in range(2):
+            line = bx.at[y, :, pl.ds(64 * k, 64)]
+            for d in range(1, 4):
+                s2[k].put(line, line, (lax.rem(y + d, 4) * 4 + x) * NZC + zc, col)
+
+    @pl.when(core == 1)
+    def _():
+        for k in range(2):
+            line = bx.at[:, x, pl.ds(64 * k, 64)]
+            for d in range(1, 4):
+                s2[k].put(line, line, (y * 4 + lax.rem(x + d, 4)) * NZC + zc, col)
+
     if "prep" in r:
         r["prep"]()
     ready = []
@@ -293,7 +312,7 @@
             parts = []
             for jh in range(2):
                 at = (h // 4 * 8 + jh * 4 + pair % 4) * 8
-                parts.append(r["bx"][:, at : at + 16, :].astype(F32))
+                parts.append(bx[:, :, at : at + 16, :].reshape(16, 16, 256).astype(F32))
             for k in range(2):
                 cache[pair + k] = jnp.concatenate(
                     [p[:, 8 * k : 8 * k + 8].reshape(128, 256) for p in parts], axis=1
@@ -302,7 +321,7 @@
 
     totals = []
     for part in range(2):
-        s2[part].got(r["bx"].at[pl.ds(0, 15), pl.ds(64 * part, 64)])
+        s2[part].got(bx.at[pl.ds(0, 3), :, pl.ds(64 * part, 64)])
         for s in range(2):
             q, k, v, gate = ready[s]
             cache.clear()
@@ -333,7 +352,8 @@
 
         sc.sent(r["bo"])
         for k in range(2):
-            s2[k].sent(r["bx"].at[pl.ds(0, 15), pl.ds(64 * k, 64)])
+            s2[k].sent(bx.at[pl.ds(0, 3), :, pl.ds(64 * k, 64)])
+        near.sent(bx.at[0, pl.ds(0, 3)])
 
     return row_sent
 
@@ -349,12 +369,12 @@
     dr2=((8, 32, 256), BF),
     lg=((4, 32, 256), BF),
     rz=((8, 32, 256), BF),
-    rx=((16, 256, 256), BF),
+    rx=((4, 4, 256, 256), BF),
     wcol=((256, 1024), BF),
     bd=((32, 128, 512), BF),
     at=((32, 256, 512), BF),
 )
-COL_SEMS = ["c1a", "c1b", "c2", "d1", "d2", "lg", "rz", "rx", "rc"]
+COL_SEMS = ["c1a", "c1b", "c2", "d1", "d2", "lg", "rz", "rx", "ry", "rc"]
 
 
 def col_prep(r):
@@ -394,34 +414,51 @@
     lg.gather("col", r["lg"])
     right = nn(to_u, r["rz"][...].reshape(256, 256)).astype(BF)
     rx = r["rx"]
+    y, x = xy // 4, xy % 4
     for k in range(2):
 
         @pl.when(core == k)
         def _():
-            rx[xy, 128 * k : 128 * k + 128] = right[128 * k : 128 * k + 128]
+            rx[y, x, 128 * k : 128 * k + 128] = right[128 * k : 128 * k + 128]
 
     half = pl.ds(pl.multiple_of(core * 128, 128), 128)
     other = pl.ds(pl.multiple_of(128 - core * 128, 128), 128)
     rxs = Swap(r, "rx")
-    for g, prow, pcol in rxs.peers("xy"):
-        rxs.put(rx.at[xy, half], rx.at[xy, half], prow, pcol)
+    for d in range(1, 4):
+        to = lax.rem(y + d * core, 4) * 4 + lax.rem(x + d - d * core, 4)
+        rxs.put(rx.at[y, x, half], rx.at[y, x, half], to * NZC + zc, col)
+    rxs.got(rx.at[0, pl.ds(0, 3), pl.ds(0, 128)])
+    rys = Swap(r, "ry")
+
+    @pl.when(core == 0)
+    def _():
+        line = rx.at[y, :, pl.ds(0, 128)]
+        for d in range(1, 4):
+            rys.put(line, line, (lax.rem(y + d, 4) * 4 + x) * NZC + zc, col)
+
+    @pl.when(core == 1)
+    def _():
+        line = rx.at[:, x, pl.ds(128, 128)]
+        for d in range(1, 4):
+            rys.put(line, line, (y * 4 + lax.rem(x + d, 4)) * NZC + zc, col)
+
     lg.got(r["lg"].at[pl.ds(0, 3)])
     left = r["lg"][...].reshape(128, 256).T
     for u in range(32):
         r["at"][u] = nn(left, r["bd"][u]).astype(BF)
-    rxs.got(rx.at[pl.ds(0, 15), pl.ds(0, 128)])
+    rys.got(rx.at[pl.ds(0, 3), :, pl.ds(0, 128)])
     rc = Swap(r, "rc")
-    rc.put(rx.at[:, half], rx.at[:, half], row + 1 - 2 * core, col)
+    rc.put(rx.at[:, :, half], rx.at[:, :, half], row + 1 - 2 * core, col)
     def add(base, acc):
         for up in range(8):
             at = pl.multiple_of(base * 8 + up * 16, 16)
-            block = rx[:, pl.ds(at, 16), :].astype(F32)
+            block = rx[:, :, pl.ds(at, 16), :].reshape(16, 16, 256).astype(F32)
             for k in range(2):
                 acc = acc + nn(block[:, 8 * k : 8 * k + 8].reshape(128, 256).astype(BF), r["at"][base + 2 * up + k])
         return acc
 
     acc = add(core * 16, jnp.zeros((128, 512), F32))
-    rc.got(rx.at[:, other])
+    rc.got(rx.at[:, :, other])
     acc = add(16 - core * 16, acc)
     for i in range(4):
         r["z1"][i] = r["pairs"][i].astype(F32) + acc[:, 128 * i : 128 * i + 128] * (1.0 / 256.0)
@@ -451,8 +488,9 @@
         d2.sent(r["ds2"].at[pl.ds(0, 7)])
         lg.sent(r["lg"].at[pl.ds(0, 3)])
         rz.sent(r["rz"].at[pl.ds(0, 7)])
-        rxs.sent(rx.at[pl.ds(0, 15), pl.ds(0, 128)])
-        rc.sent(rx.at[:, half])
+        rxs.sent(rx.at[0, pl.ds(0, 3), pl.ds(0, 128)])
+        rys.sent(rx.at[pl.ds(0, 3), :, pl.ds(0, 128)])
+        rc.sent(rx.at[:, :, half])
 
     return col_sent
 

time: 179 us -> 177 us (0.989)
  Pallas kernels: 176 us -> 173 us
    pallas_call x1, Pallas kernels: 176 us -> 173 us  [run_parts(): pl.pallas_call(body, out_shape=[jax.ShapeDtypeStruct(*SHAPES[n]) for n in...]
where the time goes in v6:
time: 177 us; the launch traced here: 176 us
  Pallas kernels  173 us (98%)
  local copies, waits for them, and re-layouts  2.32 us (1%)
    pallas_call x1, Pallas kernels, run_parts(): pl.pallas_call(body, out_shape=[jax.ShapeDtypeStruct(*SHAPES[n]) for n in...  173 us

profile of v6, /device:TPU:1, one launch (start us, length us, event | category | flops | bytes accessed | tf_op | source)
XLA Modules:
  0.0 176.3 jit_solution(13560904345114820743)
XLA Ops:
  0.6 173.3 %row_col_out_inc.1 = (bf16[2,128,256]{2,1,0:T(8,128)(2,1)}, f32[4,128,128]{2,1,0:T(8,128)}) custom-call(bf16[2,128,256]{2,1,0:T(8,128)(2,1)} %bitcast.11, bf16[4,128,128]{2,1,0:T(8,128)(2,1)} %bitcast.12, bf16[256,1024]{1,0:T(8,128)(2,1)} %refs_2_.1, bf16[256,256]{1,0:T(8,128)(2,1)} %refs_3_.1, bf16[8,128]{1,0:T(8,128)(2,1)} %bitcast.15, ...), custom_call_target="tpu_custom_call" | custom-call | tf_op jit(solution)/shard_map/row_col_out_inc/pallas_call | solution.py:683
  173.9 0.0 copy-start
  174.0 1.6 copy.19
  175.6 0.0 copy-done
  175.6 0.7 copy.20
Async XLA Ops:
  173.9 1.6 copy-start

commit v7 on v6

--- a/solution.py
+++ b/solution.py
@@ -497,7 +497,7 @@
 
 def tri_scratch(t, outgoing):
     return {
-        t + "f": ((1024, 128), F32),
+        t + "f": ((1032, 128), F32),
         t + "h": ((512, 128), F32),
         t + "s2": ((64, 16, 128), BF),
         t + "r2": ((16, 4, 16, 128), BF),

time: 177 us -> 177 us (level)
  no operation moved by 1% of the time
where the time goes in v7:
time: 177 us
  Pallas kernels  174 us (98%)
  local copies, waits for them, and re-layouts  2.32 us (1%)
    pallas_call x1, Pallas kernels, run_parts(): pl.pallas_call(body, out_shape=[jax.ShapeDtypeStruct(*SHAPES[n]) for n in...  174 us

profile of v7, /device:TPU:1, one launch (start us, length us, event | category | flops | bytes accessed | tf_op | source)
XLA Modules:
  0.0 176.7 jit_solution(13231225131951041804)
XLA Ops:
  0.6 173.8 %row_col_out_inc.1 = (bf16[2,128,256]{2,1,0:T(8,128)(2,1)}, f32[4,128,128]{2,1,0:T(8,128)}) custom-call(bf16[2,128,256]{2,1,0:T(8,128)(2,1)} %bitcast.11, bf16[4,128,128]{2,1,0:T(8,128)(2,1)} %bitcast.12, bf16[256,1024]{1,0:T(8,128)(2,1)} %refs_2_.1, bf16[256,256]{1,0:T(8,128)(2,1)} %refs_3_.1, bf16[8,128]{1,0:T(8,128)(2,1)} %bitcast.15, ...), custom_call_target="tpu_custom_call" | custom-call | tf_op jit(solution)/shard_map/row_col_out_inc/pallas_call | solution.py:683
  174.4 0.0 copy-start
  174.4 1.6 copy.19
  176.0 0.0 copy-done
  176.0 0.7 copy.20
Async XLA Ops:
  174.4 1.6 copy-start
